TPU v7x, 32 devices: a whole 2x2x4 slice. The times are simulated.
32 devices in a mesh: row: 4 (over z), col: 8 (over y, x, core).
Axes of the slice: x: 2, y: 2, z: 4, core: 2. Of those that a mesh axis runs over, the one named last changes fastest.
Arguments:
- embeddings: float32 [2048, 768], P(('row', 'col'))
- labels: int32 [2048], P(('row', 'col')), may hold values from 0 to 1, as said below
- source_id: int32 [2048], P(('row', 'col')), may hold values from 0 to 2047, as said below
Outputs:
- proof: float32 [2048], P(('row', 'col'))
- mmd_value: float32 [], replicated
Inputs may be any that keep to these rules, and one draw needn't show every extreme that they name: `labels`: exactly 1024 samples carry 1. `source_id`: every sample id appears once; at a position of grid block b (positions b * 64 to (b + 1) * 64 - 1) the id's remainder modulo 64, divided by 2 and rounded down, equals b.
All inputs are finite; a program needn't handle non-finite values.
Results may differ from a plain program's by a relative error of at most 0.00007.
Values sent between devices are 32-bit elements; how exact they have to be, the bound alone decides.
No kernel may reach another device: no remote copies, remote signals or barrier semaphores. Data moves between devices by JAX's collectives and lax.ppermute only.
A program may use at most 128 MiB of HBM per device.

v0:
```python
import jax
import jax.numpy as jnp
from jax import lax
from jax.sharding import PartitionSpec as P


def kernel_sum(query_rows, query_norm, key_rows, key_sign):
    key_norm = jnp.sum(key_rows * key_rows, axis=1)
    inner_prod = lax.dot_general(
        query_rows,
        key_rows,
        (((1,), (1,)), ((), ())),
        precision=lax.Precision.HIGHEST,
        preferred_element_type=jnp.float32,
    )
    sq_dist = query_norm[:, None] + key_norm[None, :] - 2.0 * inner_prod
    kernel = jnp.exp(sq_dist * (-1.0 / 200.0))
    return jnp.dot(
        kernel, key_sign, precision=lax.Precision.HIGHEST, preferred_element_type=jnp.float32
    )


def make_adder(query_emb, query_norm, key_piece):
    return kernel_sum(query_emb, query_norm, key_piece[0], key_piece[1])


def local(embeddings, labels, source_id):
    row_count = lax.axis_size("row")
    col_count = lax.axis_size("col")
    blocks_total = row_count * col_count
    block_rows = embeddings.shape[0]
    feature_dim = embeddings.shape[1]
    per_peer = block_rows // blocks_total
    half_count = block_rows * blocks_total // 2
    factor = 1000.0 / half_count
    set_sign = (1 - 2 * labels).astype(jnp.float32)
    picked = source_id // block_rows * per_peer + source_id % per_peer
    arrived, arrived_sign = (
        lax.all_to_all(
            embeddings.reshape(blocks_total, per_peer, feature_dim),
            ("row", "col"),
            split_axis=0,
            concat_axis=0,
            tiled=True,
        ),
        lax.all_to_all(
            set_sign.reshape(blocks_total, per_peer),
            ("row", "col"),
            split_axis=0,
            concat_axis=0,
            tiled=True,
        ),
    )
    local_emb = arrived.reshape(block_rows, feature_dim)[picked]
    local_sign = arrived_sign.reshape(block_rows)[picked]
    query_emb, query_sign = (
        lax.all_gather(local_emb, "col", axis=0, tiled=True),
        lax.all_gather(local_sign, "col", axis=0, tiled=True),
    )
    query_norm = jnp.sum(query_emb * query_emb, axis=1)
    partial_value = make_adder(
        query_emb,
        query_norm,
        (
            lax.all_gather(local_emb, "row", axis=0, tiled=True),
            lax.all_gather(local_sign, "row", axis=0, tiled=True),
        ),
    )
    scaled = partial_value * factor
    summed = lax.psum_scatter(scaled, "col", scatter_dimension=0, tiled=True)
    mmd_total = lax.psum(jnp.sum(local_sign * summed), ("row", "col"))
    mmd_value = mmd_total * (1.0 / half_count)
    return (summed, mmd_value)


def solution(mesh):
    return jax.shard_map(
        local,
        mesh=mesh,
        in_specs=(P(("row", "col"), None), P(("row", "col")), P(("row", "col"))),
        out_specs=(P(("row", "col")), P()),
        check_vma=False,
    )
```

profile of v0, /device:TPU:0, one launch (start us, length us, event | category | flops | bytes accessed | tf_op | source)
XLA Modules:
  0.0 130.0 jit_solution(11955753553643263215)
XLA Ops:
  7.2 0.0 copy-start.3
  7.2 0.0 copy-start.2
  7.2 0.0 copy-start.1
  7.2 1.7 %reshape.20 = f32[32,2,768]{2,1,0:T(2,128)} reshape(f32[64,768]{1,0:T(8,128)} %param.3) | data formatting | bytes 393216 | tf_op jit(solution)/shard_map/reshape | solution.py:40
  8.9 7.3 %all-to-all-start = ((f32[32,2,768]{2,1,0:T(2,128)}), f32[32,2,768]{2,1,0:T(2,128)S(1)}, u32[]{:S(2)}, u32[]{:S(2)}) async-start(f32[32,2,768]{2,1,0:T(2,128)} %reshape.20), calls=%async_computation | async-start | bytes 393216 | tf_op jit(solution)/shard_map/all_to_all | solution.py:39
  16.2 0.0 all-gather.5.cloned.1.call-start
  16.3 0.7 compare_select_fusion
  17.0 8.2 %all-to-all-done = f32[32,2,768]{2,1,0:T(2,128)S(1)} async-done(((f32[32,2,768]{2,1,0:T(2,128)}), f32[32,2,768]{2,1,0:T(2,128)S(1)}, u32[]{:S(2)}, u32[]{:S(2)}) %all-to-all-start) | async-done | bytes 196640 | tf_op jit(solution)/shard_map/all_to_all | solution.py:39
  25.1 0.1 reshape.21
  25.2 1.3 %gather_fusion = f32[64,768]{1,0:T(8,128)} fusion(f32[64,768]{1,0:T(8,128)S(1)} %reshape.21, s32[1024]{0:T(1024)S(1)} %pad_clamp_fusion), kind=kCustom, calls=%fused_computation | custom fusion | bytes 393472 | tf_op jit(solution)/shard_map/gather | solution.py:54
  26.6 0.0 all-gather.5.cloned.1.call-update
  26.6 0.7 all_to_all.10
  27.3 2.7 %all-to-all-start.1 = ((f32[32,1,2]{2,1,0:T(1,128)}), f32[32,1,2]{2,1,0:T(1,128)S(1)}, u32[]{:S(2)}, u32[]{:S(2)}) async-start(f32[32,1,2]{2,1,0:T(1,128)} %bitcast), calls=%async_computation.1 | async-start | bytes 32768 | tf_op jit(solution)/shard_map/all_to_all | solution.py:46
  30.1 0.6 dynamic-slice
  31.3 0.6 dynamic-slice.1
  32.6 4.6 %all-to-all-done.1 = f32[32,1,2]{2,1,0:T(1,128)S(1)} async-done(((f32[32,1,2]{2,1,0:T(1,128)}), f32[32,1,2]{2,1,0:T(1,128)S(1)}, u32[]{:S(2)}, u32[]{:S(2)}) %all-to-all-start.1) | async-done | bytes 288 | tf_op jit(solution)/shard_map/all_to_all | solution.py:46
  37.2 0.5 broadcast.37
  37.7 0.7 reduce.3
  38.4 0.1 reshape.22
  38.5 0.8 gather_fusion.1
  39.3 0.2 dynamic-update-slice
  39.5 8.9 %all-reduce = f32[256]{0:T(256)S(1)} all-reduce(f32[256]{0:T(256)S(1)} %dynamic-update-slice), channel_id=4, replica_groups=mesh['row'=4,'col'=8] {'row'}, use_global_device_ids=true, to_apply=%add | all-reduce | flops 256 | bytes 2048
  48.5 17.9 %all-gather.1 = f32[256,768]{1,0:T(8,128)S(1)} all-gather(f32[64,768]{1,0:T(8,128)} %gather_fusion), channel_id=3, replica_groups=mesh['row'=4,'col'=8] {'row'}, dimensions={0}, use_global_device_ids=true | all-gather | bytes 983040 | tf_op jit(solution)/shard_map/all_gather | solution.py:65
  66.4 0.1 multiply_reduce_fusion.1
  66.5 0.0 all-gather.5.cloned.1.call-done
  66.5 1.7 %multiply_reduce_fusion = f32[512]{0:T(512)S(1)} fusion(f32[512,768]{1,0:T(8,128)} %all-gather.5.cloned.1.call-done), kind=kLoop, calls=%fused_computation.2 | loop fusion | flops 785920 | bytes 1574912 | tf_op jit(solution)/shard_map/reduce_sum | solution.py:60
  68.2 0.2 copy-done
  68.4 1.5 %fusion.2 = f32[512,256]{1,0:T(8,128)S(1)} fusion(f32[512,768]{1,0:T(8,128)S(1)} %copy-done, f32[256,768]{1,0:T(8,128)S(1)} %all-gather.1, f32[256]{0:T(256)S(1)} %multiply_reduce_fusion.1, f32[512]{0:T(512)S(1)} %multiply_reduce_fusion), kind=kOutput, calls=%fused_computation.6 | convolution fusion | flops 1208483840 | bytes 2886656 | tf_op jit(solution)/shard_map/dot_general | solution.py:9
  69.9 0.5 fusion.4
  70.4 11.8 %all-reduce.1 = f32[512]{0:T(512)S(1)} all-reduce(f32[512]{0:T(512)S(1)} %broadcast_multiply_fusion), channel_id=5, replica_groups=mesh['row'=4,'col'=8] {'col'}, use_global_device_ids=true, to_apply=%region_2.3.clone | all-reduce | flops 512 | bytes 4096
  82.2 1.2 multiply_reduce_fusion.2
  83.4 37.9 %psum.7 = f32[]{:T(128)} all-reduce(f32[]{:T(128)} %get-tuple-element.2), channel_id=1, replica_groups=mesh['row'=4,'col'=8] {'row','col'}, use_global_device_ids=true, to_apply=%region_4.5 | all-reduce | flops 1 | bytes 8 | tf_op jit(solution)/shard_map/psum | solution.py:71
  (8 shorter events, 0.0 us)
Async XLA Ops:
  7.2 22.9 %copy-start.3 = (u32[32]{0:T(128)S(1)}, u32[32]{0:T(128)}, u32[]{:S(2)}) copy-start(u32[32]{0:T(128)} %constant.46) | copy-start | bytes 388
  7.2 24.2 %copy-start.2 = (u32[32]{0:T(128)S(1)}, u32[32]{0:T(128)}, u32[]{:S(2)}) copy-start(u32[32]{0:T(128)} %constant.52) | copy-start | bytes 388
  7.2 19.4 %copy-start.1 = (s32[64]{0:T(128)S(1)}, s32[64]{0:T(128)}, u32[]{:S(2)}) copy-start(s32[64]{0:T(128)} %param.4) | copy-start | bytes 772
  8.9 16.2 %all-to-all-start = ((f32[32,2,768]{2,1,0:T(2,128)}), f32[32,2,768]{2,1,0:T(2,128)S(1)}, u32[]{:S(2)}, u32[]{:S(2)}) async-start(f32[32,2,768]{2,1,0:T(2,128)} %reshape.20), calls=%async_computation | async-start | bytes 393216 | tf_op jit(solution)/shard_map/all_to_all | solution.py:39
  16.2 50.3 %all-gather.5.cloned.1.call-start = ((), (), s32[]{:S(2)}) async-start(), calls=%async_computation.2 | async-start | bytes 1769472 | tf_op jit(solution)/shard_map/all_gather | solution.py:57
  27.3 9.9 %all-to-all-start.1 = ((f32[32,1,2]{2,1,0:T(1,128)}), f32[32,1,2]{2,1,0:T(1,128)S(1)}, u32[]{:S(2)}, u32[]{:S(2)}) async-start(f32[32,1,2]{2,1,0:T(1,128)} %bitcast), calls=%async_computation.1 | async-start | bytes 32768 | tf_op jit(solution)/shard_map/all_to_all | solution.py:46
  66.5 1.9 %copy-start = (f32[512,768]{1,0:T(8,128)S(1)}, f32[512,768]{1,0:T(8,128)}, u32[]{:S(2)}) copy-start(f32[512,768]{1,0:T(8,128)} %all-gather.5.cloned.1.call-done) | copy-start | bytes 4718596
Sparse Core Ops, SparseCore 0:
  26.7 23.7 all-gather.4
where the time goes:
time: 130 us
  blocking collectives  76.5 us (59%)
  between operations  17.2 us (13%)
  waiting for transfers between devices  12.8 us (10%)
  starting transfers between devices  10.1 us (8%)
  local copies, waits for them, and re-layouts  6.89 us (5%)
  other arithmetic  4.39 us (3%)
  matrix products  2 us (2%)
    psum x1, blocking collectives, local(): mmd_total = lax.psum(jnp.sum(local_sign * summed), ('row', 'col'))  37.9 us
    unnamed x2, blocking collectives  20.7 us
    all_gather x1, blocking collectives, local(): lax.all_gather(local_emb, 'row', axis=0, tiled=True)  17.9 us
    all_to_all x1, waiting for transfers between devices, local(): lax.all_to_all(embeddings.reshape(blocks_total, per_peer, feature_dim), (...  8.15 us
    all_to_all x1, starting transfers between devices, local(): lax.all_to_all(embeddings.reshape(blocks_total, per_peer, feature_dim), (...  7.3 us
    all_to_all x1, waiting for transfers between devices, local(): lax.all_to_all(set_sign.reshape(blocks_total, per_peer), ('row', 'col'),...  4.64 us
    all_to_all x1, starting transfers between devices, local(): lax.all_to_all(set_sign.reshape(blocks_total, per_peer), ('row', 'col'),...  2.71 us
  transfers between devices with their start and end apart: 3, of which 2 were waited for; matrix products, arithmetic and copies ran while one was open for 3% of the time, Pallas kernels for 0%

commit v1 on v0

v1 whole, which is shorter than its diff:
```python
import functools

import jax
import jax.numpy as jnp
from jax import lax
from jax.experimental import pallas as pl
from jax.experimental.pallas import tpu as pltpu
from jax.sharding import PartitionSpec as P

LANES = 128
SUBLANES = 8
GROUP_ROWS = 256
PLANES = 4
CORES = 2
ROUND_A = {2: 0, 3: 1, 1: 2, 0: 3}
ROUND_B = {0: 1, 3: 2, 1: 0, 2: 3}
CROSSING = (1, 2)
FAR_BLOCKS = 3
MIB = 1024 * 1024
NT_DIMS = (((1,), (1,)), ((), ()))
NN_DIMS = (((1,), (0,)), ((), ()))


def int_div(value, divisor):
    if divisor & (divisor - 1) == 0:
        return lax.shift_right_logical(value, divisor.bit_length() - 1)
    return value // divisor


def int_mod(value, divisor):
    if divisor & (divisor - 1) == 0:
        return value & (divisor - 1)
    return value % divisor


class Layout:
    def __init__(self, row_count, col_count):
        self.core_in_row = row_count == PLANES * CORES
        self.places = col_count if self.core_in_row else col_count // CORES
        self.devices = row_count * col_count

    def flat(self, plane, place, core):
        if self.core_in_row:
            return (plane * CORES + core) * self.places + place
        return (plane * self.places + place) * CORES + core

    def parts(self, flat):
        if self.core_in_row:
            place, rest = int_mod(flat, self.places), int_div(flat, self.places)
            return int_div(rest, CORES), place, int_mod(rest, CORES)
        core, rest = int_mod(flat, CORES), int_div(flat, CORES)
        return int_div(rest, self.places), int_mod(rest, self.places), core

    def here(self):
        row, col = lax.axis_index("row"), lax.axis_index("col")
        if self.core_in_row:
            return int_div(row, CORES), col, int_mod(row, CORES)
        return row, int_div(col, CORES), int_mod(col, CORES)

    def pairs(self, target):
        result = []
        for plane in range(PLANES):
            for place in range(self.places):
                for core in range(CORES):
                    goal = target(plane, place, core)
                    result.append((self.flat(plane, place, core), self.flat(*goal)))
        return sorted(result)


def split2(value):
    high = value.astype(jnp.bfloat16)
    return high, (value - high.astype(jnp.float32)).astype(jnp.bfloat16)


def split3(value):
    high = value.astype(jnp.bfloat16)
    rest = value - high.astype(jnp.float32)
    mid = rest.astype(jnp.bfloat16)
    low = (rest - mid.astype(jnp.float32)).astype(jnp.bfloat16)
    return high, mid, low


def bf16_dot(left, right, dims):
    return lax.dot_general(left, right, dims, preferred_element_type=jnp.float32)


def pack_kernel(emb_ref, label_ref, id_ref, out_ref, id_out_ref):
    samples, width = emb_ref.shape
    id_out_ref[...] = id_ref[...]
    emb = emb_ref[...]
    norm = lax.dot_general(
        jnp.ones((SUBLANES, width), jnp.float32),
        emb * emb,
        NT_DIMS,
        precision=lax.Precision.HIGHEST,
        preferred_element_type=jnp.float32,
    )
    sign = (1 - 2 * label_ref[...]).astype(jnp.float32)
    for chunk in range(width // LANES):
        out_ref[pl.ds(chunk * samples, samples), :] = emb[:, chunk * LANES : (chunk + 1) * LANES]
    base = samples * (width // LANES)
    row = lax.broadcasted_iota(jnp.int32, (SUBLANES, samples), 0)
    both = jnp.where(row == 0, sign, norm)
    for start in range(0, samples, LANES):
        lanes = min(LANES, samples - start)
        place = base + start // LANES * SUBLANES
        if lanes < LANES:
            out_ref[pl.ds(place, SUBLANES), :] = jnp.zeros((SUBLANES, LANES), jnp.float32)
        out_ref[pl.ds(place, SUBLANES), pl.ds(0, lanes)] = both[:, start : start + lanes]


def stage(ref, scratch, start, samples, chunks):
    for chunk in range(chunks):
        value = ref[pl.ds(chunk * samples, samples), :]
        for part, piece in zip(scratch, split2(value)):
            part[pl.ds(start, samples), pl.ds(chunk * LANES, LANES)] = piece


def tail_rows(refs, samples, chunks):
    pieces = []
    for ref in refs:
        for start in range(0, samples, LANES):
            lanes = min(LANES, samples - start)
            place = samples * chunks + start // LANES * SUBLANES
            pieces.append(ref[pl.ds(place, SUBLANES), pl.ds(0, lanes)])
    return jnp.concatenate(pieces, axis=1)


def main_kernel(samples, chunks, layout, *refs):
    places = layout.places
    queries = refs[:places]
    keys = (refs[0],) + refs[places : places + 4]
    out_ref = refs[places + 4]
    key_parts = refs[places + 5 : places + 7]
    query_parts = refs[places + 7 : places + 9]
    tail_ref = refs[places + 9]
    _, me_place, me_core = layout.here()
    rows = places * samples
    group = min(GROUP_ROWS, rows)
    blocks = group // samples
    near = CORES * samples
    for place, ref in enumerate(keys):
        stage(ref, key_parts, place * samples, samples, chunks)
    for place, ref in enumerate(queries):
        stage(ref, query_parts, place * samples, samples, chunks)
    key_tail = tail_rows(keys, samples, chunks)
    key_sign, key_norm = key_tail[0:1, :], key_tail[1:2, :]
    tail_ref[...] = jnp.transpose(tail_rows(queries, samples, chunks))
    lane = lax.broadcasted_iota(jnp.int32, (samples, LANES), 1)

    def one_group(index, carry):
        result, total, column = carry
        start = pl.multiple_of(index * group, group)
        high, mid = (part[pl.ds(start, group), :] for part in query_parts)
        key_high, key_mid = (part[...] for part in key_parts)
        inner = bf16_dot(mid, key_mid, NT_DIMS)
        inner = inner + (bf16_dot(high, key_mid, NT_DIMS) + bf16_dot(mid, key_high, NT_DIMS))
        inner = inner + bf16_dot(high, key_high, NT_DIMS)
        sign = tail_ref[pl.ds(start, group), 0:1]
        norm = tail_ref[pl.ds(start, group), 1:2]
        sq_dist = norm + key_norm - 2.0 * inner
        kernel = jnp.exp(sq_dist * (-1.0 / 200.0))
        signed = kernel * key_sign
        near_sums = jnp.sum(signed[:, :near], axis=1, keepdims=True)
        far_sums = jnp.sum(signed[:, near:], axis=1, keepdims=True)
        sums = near_sums + far_sums
        total = total + jnp.sum(sign * (sums + far_sums), axis=0, keepdims=True)
        column = column + jnp.sum(kernel[:, near:] * sign, axis=0, keepdims=True)
        for place in range(blocks):
            owner = me_place ^ (index * blocks + place)
            result = jnp.where(
                lane == owner, sums[place * samples : (place + 1) * samples, :], result
            )
        return result, total, column

    carry = (
        jnp.zeros((samples, LANES), jnp.float32),
        jnp.zeros((1, 1), jnp.float32),
        jnp.zeros((1, FAR_BLOCKS * samples), jnp.float32),
    )
    if rows == group:
        carry = one_group(0, carry)
    else:
        carry = lax.fori_loop(0, rows // group, one_group, carry)
    result, total, column = carry
    column = jnp.concatenate([column, jnp.zeros((1, samples), jnp.float32)], axis=1)
    column = jnp.transpose(jnp.broadcast_to(column, (SUBLANES, (FAR_BLOCKS + 1) * samples)))
    for place, offset in enumerate((me_core, 1 - me_core, 2)):
        result = jnp.where(
            lane == places + offset, column[place * samples : (place + 1) * samples, 0:1], result
        )
    out_ref[...] = jnp.where(lane == places + 4, total, result)


def last_kernel(layout, samples, per_peer, factor, half_count, got_ref, id_ref, proof_ref, mmd_ref):
    got = got_ref[...]
    ids = id_ref[...]
    places = layout.places
    plane, place, core = layout.parts(int_div(ids, samples))
    slot = int_mod(ids, per_peer)
    targets = jnp.concatenate(
        [place, places + core, jnp.full(core.shape, places + 2, jnp.int32)], axis=1
    )
    lane_of = lax.broadcasted_iota(jnp.int32, (LANES, 3 * samples), 0)
    picks = jnp.where(lane_of == targets, 1.0, 0.0).astype(jnp.bfloat16)
    high, mid, low = split3(got)
    picked = bf16_dot(high, picks, NN_DIMS) + (
        bf16_dot(mid, picks, NN_DIMS) + bf16_dot(low, picks, NN_DIMS)
    )
    row = lax.broadcasted_iota(jnp.int32, (samples, samples), 0)
    src_plane, src_place, src_core = layout.parts(int_div(row, per_peer))
    right_slot = int_mod(row, per_peer) == slot
    keep_row = right_slot & (src_plane == plane) & (src_core == core)
    right_place = right_slot & (src_place == place)

    def sent_to(table):
        goal = jnp.full(plane.shape, -1, jnp.int32)
        for source, target in table.items():
            goal = jnp.where(plane == source, target, goal)
        return goal

    keep_a = right_place & (src_plane == sent_to(ROUND_A))
    crossing = (plane == CROSSING[0]) | (plane == CROSSING[1])
    keep_b = right_place & (src_plane == sent_to(ROUND_B))
    keep_b = keep_b & (src_core == jnp.where(crossing, 1 - core, core))
    sums = jnp.where(keep_row, picked[:, :samples], 0.0)
    sums = sums + jnp.where(keep_a, picked[:, samples : 2 * samples], 0.0)
    sums = sums + jnp.where(keep_b, picked[:, 2 * samples :], 0.0)
    proof_ref[...] = jnp.sum(sums, axis=0, keepdims=True) * factor
    row = lax.broadcasted_iota(jnp.int32, (samples, LANES), 0)
    lane = lax.broadcasted_iota(jnp.int32, (samples, LANES), 1)
    is_total = (lane == places + 4) & (int_mod(row, per_peer) == 0)
    total = jnp.sum(jnp.where(is_total, got, 0.0), axis=(0, 1), keepdims=True)
    mmd_ref[...] = total * factor * (1.0 / half_count)


def in_vmem(array):
    return pltpu.with_memory_space_constraint(array, pltpu.VMEM)


def in_hbm(array):
    return pltpu.with_memory_space_constraint(array, pltpu.HBM)


def vmem_specs(count):
    return [pl.BlockSpec(memory_space=pltpu.VMEM)] * count


def local(embeddings, labels, source_id):
    layout = Layout(lax.axis_size("row"), lax.axis_size("col"))
    places = layout.places
    samples, width = embeddings.shape
    chunks = width // LANES
    per_peer = samples // layout.devices
    half_count = samples * layout.devices // 2
    factor = 1000.0 / half_count
    tiles = -(-samples // LANES)
    pack_rows = samples * chunks + tiles * SUBLANES
    key_rows = (CORES + FAR_BLOCKS) * samples
    query_rows = places * samples
    block_bytes = pack_rows * LANES * 4
    work_bytes = (key_rows + query_rows) * width * 6 + 8 * GROUP_ROWS * key_rows * 4
    params = pltpu.CompilerParams(vmem_limit_bytes=work_bytes + 4 * MIB)

    packed, ids = pl.pallas_call(
        pack_kernel,
        out_shape=(
            pltpu.VMEM((pack_rows, LANES), jnp.float32),
            pltpu.VMEM((1, samples), jnp.int32),
        ),
        in_specs=vmem_specs(3),
        out_specs=tuple(vmem_specs(2)),
        compiler_params=pltpu.CompilerParams(vmem_limit_bytes=4 * block_bytes + 4 * MIB),
        name="pack_block",
    )(
        in_hbm(embeddings),
        in_hbm(labels.reshape(1, samples)),
        in_hbm(source_id.reshape(1, samples)),
    )

    def send(block, target):
        return lax.ppermute(block, ("row", "col"), layout.pairs(target))

    def round_a(plane, place, core):
        return (ROUND_A[plane], place, core)

    def round_b(plane, place, core):
        return (ROUND_B[plane], place, 1 - core if plane in CROSSING else core)

    def to_place(step):
        return lambda plane, place, core: (plane, place ^ step, core)

    def to_core(plane, place, core):
        return (plane, place, 1 - core)

    in_plane = [send(packed, to_place(step)) for step in range(1, places)]
    far_b = send(packed, round_b)
    far_a = send(packed, round_a)
    far_a_other = send(far_a, to_core)
    late, *_ = lax.optimization_barrier((packed, in_plane[-1], far_a))
    near = send(late, to_core)

    blocks = [packed, *in_plane, near, far_a, far_a_other, far_b]
    partial = pl.pallas_call(
        functools.partial(main_kernel, samples, chunks, layout),
        out_shape=pltpu.VMEM((samples, LANES), jnp.float32),
        in_specs=vmem_specs(len(blocks)),
        out_specs=pl.BlockSpec(memory_space=pltpu.VMEM),
        scratch_shapes=[pltpu.VMEM((key_rows, width), jnp.bfloat16)] * 2
        + [pltpu.VMEM((query_rows, width), jnp.bfloat16)] * 2
        + [pltpu.VMEM((query_rows, SUBLANES), jnp.float32)],
        compiler_params=params,
        name="kernel_sums",
    )(*[in_vmem(block) for block in blocks])

    got = lax.all_to_all(partial, ("row", "col"), split_axis=0, concat_axis=0, tiled=True)

    proof, mmd = pl.pallas_call(
        functools.partial(last_kernel, layout, samples, per_peer, factor, half_count),
        out_shape=(
            jax.ShapeDtypeStruct((1, samples), jnp.float32),
            jax.ShapeDtypeStruct((1, 1), jnp.float32),
        ),
        in_specs=vmem_specs(2),
        out_specs=tuple(vmem_specs(2)),
        compiler_params=pltpu.CompilerParams(vmem_limit_bytes=16 * MIB),
        name="pick_proof",
    )(in_vmem(got), in_vmem(ids))
    return proof.reshape(samples), mmd.reshape(())


def solution(mesh):
    return jax.shard_map(
        local,
        mesh=mesh,
        in_specs=(P(("row", "col"), None), P(("row", "col")), P(("row", "col"))),
        out_specs=(P(("row", "col")), P()),
        check_vma=False,
    )
```

time: 130 us -> 30.5 us (0.23)
  blocking collectives: 76.5 us -> 9.29 us
  between operations: 17.2 us -> 0.66 us
  local copies, waits for them, and re-layouts: 6.89 us -> 0 us
  waiting for transfers between devices: 12.8 us -> 7.93 us
  other arithmetic: 4.39 us -> 0 us
  Pallas kernels: 0 us -> 3.37 us
  matrix products: 2 us -> 0 us
    psum x1 -> x0, blocking collectives: 37.9 us -> none  [local(): mmd_total = lax.psum(jnp.sum(local_sign * summed), ('row', 'col'))]
    unnamed x2 -> x0, blocking collectives: 20.7 us -> none
    all_gather x1 -> x0, blocking collectives: 17.9 us -> none  [local(): lax.all_gather(local_emb, 'row', axis=0, tiled=True)]
    all_to_all x2 -> x0, waiting for transfers between devices: 12.8 us -> none  [the longest x1 8.15 us: local(): lax.all_to_all(embeddings.reshape(blocks_total, per_peer, feature_dim), (...]
    all_to_all x2 -> x0, starting transfers between devices: 10 us -> none  [the longest x1 7.3 us: local(): lax.all_to_all(embeddings.reshape(blocks_total, per_peer, feature_dim), (...]
    all_to_all x0 -> x1, blocking collectives: none -> 9.29 us  [local(): lax.all_to_all(partial, ('row', 'col'), split_axis=0, concat_axis=0, tile...]
    ppermute x0 -> x7, starting transfers between devices: none -> 9.06 us  [send(): return lax.ppermute(block, ('row', 'col'), layout.pairs(target))]
    ppermute x0 -> x7, waiting for transfers between devices: none -> 7.93 us  [send(): return lax.ppermute(block, ('row', 'col'), layout.pairs(target))]
  transfers between devices with their start and end apart: 3 -> 7, of which waited for: 2 -> 3; matrix products, arithmetic and copies ran while one was open for 3% -> 0% of each run, Pallas kernels for 0% -> 0%
where the time goes in v1:
time: 30.5 us; the launch traced here: 30.3 us
  blocking collectives  9.29 us (30%)
  starting transfers between devices  9.06 us (30%)
  waiting for transfers between devices  7.93 us (26%)
  Pallas kernels  3.37 us (11%)
  between operations  0.66 us (2%)
    all_to_all x1, blocking collectives, local(): lax.all_to_all(partial, ('row', 'col'), split_axis=0, concat_axis=0, tile...  9.29 us
    ppermute x7, starting transfers between devices, send(): return lax.ppermute(block, ('row', 'col'), layout.pairs(target))  9.06 us
    ppermute x7, waiting for transfers between devices, send(): return lax.ppermute(block, ('row', 'col'), layout.pairs(target))  7.93 us
    pallas_call x1, Pallas kernels, local(): pl.pallas_call(functools.partial(main_kernel, samples, chunks, layout), o...  1.32 us
    pallas_call x1, Pallas kernels, local(): pl.pallas_call(pack_kernel, out_shape=(pltpu.VMEM((pack_rows, LANES), jnp...  1.21 us
    pallas_call x1, Pallas kernels, local(): pl.pallas_call(functools.partial(last_kernel, layout, samples, per_peer,...  0.84 us
  transfers between devices with their start and end apart: 7, of which 3 were waited for; matrix products, arithmetic and copies ran while one was open for 0% of the time, Pallas kernels for 0%

profile of v1, /device:TPU:0, one launch (start us, length us, event | category | flops | bytes accessed | tf_op | source)
XLA Modules:
  0.0 30.3 jit_solution(14974789911511785364)
XLA Ops:
  0.6 1.2 %pack_block.1 = (f32[392,128]{1,0:T(8,128)S(1)}, s32[1,64]{1,0:T(1,128)S(1)}) custom-call(f32[64,768]{1,0:T(8,128)} %emb_ref.1, s32[1,64]{1,0:T(1,128)} %bitcast.8, s32[1,64]{1,0:T(1,128)} %bitcast.9), custom_call_target="tpu_custom_call" | custom-call | tf_op jit(solution)/shard_map/pack_block/pallas_call | solution.py:265
  1.8 5.1 %collective-permute-start.3 = (f32[392,128]{1,0:T(8,128)S(1)}, f32[392,128]{1,0:T(8,128)S(1)}, u32[]{:S(2)}, u32[]{:S(2)}) collective-permute-start(f32[392,128]{1,0:T(8,128)S(1)} %get-tuple-element.8.refs_0_), channel_id=1, source_target_pairs={{0,24},{1,25},{2,26},{3,27},{4,28},{5,29},{6,30},{7,31},{8,16},{9,... | collective-permute-start | bytes 602120 | tf_op jit(solution)/shard_map/ppermute | solution.py:282
  6.9 2.4 %collective-permute-start.2 = (f32[392,128]{1,0:T(8,128)S(1)}, f32[392,128]{1,0:T(8,128)S(1)}, u32[]{:S(2)}, u32[]{:S(2)}) collective-permute-start(f32[392,128]{1,0:T(8,128)S(1)} %get-tuple-element.8.refs_0_), channel_id=1, source_target_pairs={{0,6},{1,7},{2,4},{3,5},{4,2},{5,3},{6,0},{7,1},{8,14},{9,15},{10,... | collective-permute-start | bytes 602120 | tf_op jit(solution)/shard_map/ppermute | solution.py:282
  9.4 0.0 collective-permute-start.6
  9.4 0.5 %collective-permute-start.1 = (f32[392,128]{1,0:T(8,128)S(1)}, f32[392,128]{1,0:T(8,128)S(1)}, u32[]{:S(2)}, u32[]{:S(2)}) collective-permute-start(f32[392,128]{1,0:T(8,128)S(1)} %get-tuple-element.8.refs_0_), channel_id=1, source_target_pairs={{0,4},{1,5},{2,6},{3,7},{4,0},{5,1},{6,2},{7,3},{8,12},{9,13},{10,... | collective-permute-start | bytes 602120 | tf_op jit(solution)/shard_map/ppermute | solution.py:282
  9.9 0.5 %collective-permute-start = (f32[392,128]{1,0:T(8,128)S(1)}, f32[392,128]{1,0:T(8,128)S(1)}, u32[]{:S(2)}, u32[]{:S(2)}) collective-permute-start(f32[392,128]{1,0:T(8,128)S(1)} %get-tuple-element.8.refs_0_), channel_id=1, source_target_pairs={{0,2},{1,3},{2,0},{3,1},{4,6},{5,7},{6,4},{7,5},{8,10},{9,11},{10,... | collective-permute-start | bytes 602120 | tf_op jit(solution)/shard_map/ppermute | solution.py:282
  10.4 4.9 %collective-permute-done.3.refs_5_ = f32[392,128]{1,0:T(8,128)S(1)} collective-permute-done((f32[392,128]{1,0:T(8,128)S(1)}, f32[392,128]{1,0:T(8,128)S(1)}, u32[]{:S(2)}, u32[]{:S(2)}) %collective-permute-start.3) | collective-permute-done | bytes 200736 | tf_op jit(solution)/shard_map/ppermute | solution.py:282
  15.3 0.4 %collective-permute-done.2.refs_3_ = f32[392,128]{1,0:T(8,128)S(1)} collective-permute-done((f32[392,128]{1,0:T(8,128)S(1)}, f32[392,128]{1,0:T(8,128)S(1)}, u32[]{:S(2)}, u32[]{:S(2)}) %collective-permute-start.2) | collective-permute-done | bytes 200736 | tf_op jit(solution)/shard_map/ppermute | solution.py:282
  15.7 0.0 collective-permute-start.5
  15.7 0.5 %collective-permute-start.4 = (f32[392,128]{1,0:T(8,128)S(1)}, f32[392,128]{1,0:T(8,128)S(1)}, u32[]{:S(2)}, u32[]{:S(2)}) collective-permute-start(f32[392,128]{1,0:T(8,128)S(1)} %get-tuple-element.8.refs_0_), channel_id=1, source_target_pairs={{0,1},{1,0},{2,3},{3,2},{4,5},{5,4},{6,7},{7,6},{8,9},{9,8},{10,11... | collective-permute-start | bytes 602120 | tf_op jit(solution)/shard_map/ppermute | solution.py:282
  16.2 2.6 %collective-permute-done.6.refs_7_ = f32[392,128]{1,0:T(8,128)S(1)} collective-permute-done((f32[392,128]{1,0:T(8,128)S(1)}, f32[392,128]{1,0:T(8,128)S(1)}, u32[]{:S(2)}, u32[]{:S(2)}) %collective-permute-start.6) | collective-permute-done | bytes 200736 | tf_op jit(solution)/shard_map/ppermute | solution.py:282
  18.8 0.0 collective-permute-done.1.refs_2_
  18.8 0.0 collective-permute-done.refs_1_
  18.8 0.0 collective-permute-done.5.refs_6_
  18.8 0.0 collective-permute-done.4.refs_4_
  18.9 1.3 %kernel_sums.1 = f32[64,128]{1,0:T(8,128)S(1)} custom-call(f32[392,128]{1,0:T(8,128)S(1)} %get-tuple-element.8.refs_0_, f32[392,128]{1,0:T(8,128)S(1)} %collective-permute-done.refs_1_, f32[392,128]{1,0:T(8,128)S(1)} %collective-permute-done.1.refs_2_, f32[392,128]{1,0:T(8,128)S(1)} %collective-permute-done.2.refs_3_, ...), custom_call_target="tpu_custom_call" | custom-call | tf_op jit(solution)/shard_map/kernel_sums/pallas_call | solution.py:304
  20.2 9.3 %all_to_all.11 = f32[32,2,128]{2,1,0:T(2,128)S(1)} all-to-all(f32[32,2,128]{2,1,0:T(2,128)S(1)} %bitcast.6), channel_id=1, replica_groups=mesh['row'=4,'col'=8] {'row','col'}, dimensions={0} | all-to-all | bytes 65536 | tf_op jit(solution)/shard_map/all_to_all | solution.py:316
  29.5 0.8 %pick_proof.1 = (f32[1,64]{1,0:T(1,128)}, f32[1,1]{1,0:T(1,128)}) custom-call(f32[64,128]{1,0:T(8,128)S(1)} %bitcast.7, s32[1,64]{1,0:T(1,128)S(1)} %get-tuple-element.9.id_ref), custom_call_target="tpu_custom_call" | custom-call | tf_op jit(solution)/shard_map/pick_proof/pallas_call | solution.py:318
Async XLA Ops:
  1.8 13.4 %collective-permute-start.3 = (f32[392,128]{1,0:T(8,128)S(1)}, f32[392,128]{1,0:T(8,128)S(1)}, u32[]{:S(2)}, u32[]{:S(2)}) collective-permute-start(f32[392,128]{1,0:T(8,128)S(1)} %get-tuple-element.8.refs_0_), channel_id=1, source_target_pairs={{0,24},{1,25},{2,26},{3,27},{4,28},{5,29},{6,30},{7,31},{8,16},{9,... | collective-permute-start | bytes 602120 | tf_op jit(solution)/shard_map/ppermute | solution.py:282
  6.9 8.8 %collective-permute-start.2 = (f32[392,128]{1,0:T(8,128)S(1)}, f32[392,128]{1,0:T(8,128)S(1)}, u32[]{:S(2)}, u32[]{:S(2)}) collective-permute-start(f32[392,128]{1,0:T(8,128)S(1)} %get-tuple-element.8.refs_0_), channel_id=1, source_target_pairs={{0,6},{1,7},{2,4},{3,5},{4,2},{5,3},{6,0},{7,1},{8,14},{9,15},{10,... | collective-permute-start | bytes 602120 | tf_op jit(solution)/shard_map/ppermute | solution.py:282
  9.4 9.5 %collective-permute-start.6 = (f32[392,128]{1,0:T(8,128)S(1)}, f32[392,128]{1,0:T(8,128)S(1)}, u32[]{:S(2)}, u32[]{:S(2)}) collective-permute-start(f32[392,128]{1,0:T(8,128)S(1)} %get-tuple-element.8.refs_0_), channel_id=1, source_target_pairs={{0,8},{1,9},{2,10},{3,11},{4,12},{5,13},{6,14},{7,15},{8,1},{9,0},... | collective-permute-start | bytes 602120 | tf_op jit(solution)/shard_map/ppermute | solution.py:282
  9.4 9.5 %collective-permute-start.1 = (f32[392,128]{1,0:T(8,128)S(1)}, f32[392,128]{1,0:T(8,128)S(1)}, u32[]{:S(2)}, u32[]{:S(2)}) collective-permute-start(f32[392,128]{1,0:T(8,128)S(1)} %get-tuple-element.8.refs_0_), channel_id=1, source_target_pairs={{0,4},{1,5},{2,6},{3,7},{4,0},{5,1},{6,2},{7,3},{8,12},{9,13},{10,... | collective-permute-start | bytes 602120 | tf_op jit(solution)/shard_map/ppermute | solution.py:282
  9.9 9.0 %collective-permute-start = (f32[392,128]{1,0:T(8,128)S(1)}, f32[392,128]{1,0:T(8,128)S(1)}, u32[]{:S(2)}, u32[]{:S(2)}) collective-permute-start(f32[392,128]{1,0:T(8,128)S(1)} %get-tuple-element.8.refs_0_), channel_id=1, source_target_pairs={{0,2},{1,3},{2,0},{3,1},{4,6},{5,7},{6,4},{7,5},{8,10},{9,11},{10,... | collective-permute-start | bytes 602120 | tf_op jit(solution)/shard_map/ppermute | solution.py:282
  15.7 3.1 %collective-permute-start.5 = (f32[392,128]{1,0:T(8,128)S(1)}, f32[392,128]{1,0:T(8,128)S(1)}, u32[]{:S(2)}, u32[]{:S(2)}) collective-permute-start(f32[392,128]{1,0:T(8,128)S(1)} %collective-permute-done.3.refs_5_), channel_id=1, source_target_pairs={{0,1},{1,0},{2,3},{3,2},{4,5},{5,4},{6,7},{7,6},{8,9},{9,8},{10,11... | collective-permute-start | bytes 602120 | tf_op jit(solution)/shard_map/ppermute | solution.py:282
  15.7 3.1 %collective-permute-start.4 = (f32[392,128]{1,0:T(8,128)S(1)}, f32[392,128]{1,0:T(8,128)S(1)}, u32[]{:S(2)}, u32[]{:S(2)}) collective-permute-start(f32[392,128]{1,0:T(8,128)S(1)} %get-tuple-element.8.refs_0_), channel_id=1, source_target_pairs={{0,1},{1,0},{2,3},{3,2},{4,5},{5,4},{6,7},{7,6},{8,9},{9,8},{10,11... | collective-permute-start | bytes 602120 | tf_op jit(solution)/shard_map/ppermute | solution.py:282

commit v2 on v1

--- a/solution.py
+++ b/solution.py
@@ -109,11 +109,11 @@
         out_ref[pl.ds(place, SUBLANES), pl.ds(0, lanes)] = both[:, start : start + lanes]
 
 
-def stage(ref, scratch, start, samples, chunks):
+def stage(ref, scratch, start, middle, samples, chunks):
     for chunk in range(chunks):
         value = ref[pl.ds(chunk * samples, samples), :]
-        for part, piece in zip(scratch, split2(value)):
-            part[pl.ds(start, samples), pl.ds(chunk * LANES, LANES)] = piece
+        for offset, piece in zip((0, middle), split2(value)):
+            scratch[pl.ds(offset + start, samples), pl.ds(chunk * LANES, LANES)] = piece
 
 
 def tail_rows(refs, samples, chunks):
@@ -126,68 +126,72 @@
     return jnp.concatenate(pieces, axis=1)
 
 
+def as_columns(rows):
+    count = rows.shape[1]
+    fill = -count % LANES
+    if fill:
+        rows = jnp.concatenate([rows, jnp.zeros((SUBLANES, fill), jnp.float32)], axis=1)
+    return jnp.transpose(rows)[:count]
+
+
 def main_kernel(samples, chunks, layout, *refs):
     places = layout.places
     queries = refs[:places]
     keys = (refs[0],) + refs[places : places + 4]
-    out_ref = refs[places + 4]
-    key_parts = refs[places + 5 : places + 7]
-    query_parts = refs[places + 7 : places + 9]
-    tail_ref = refs[places + 9]
+    out_ref, key_parts, query_parts, tail_ref = refs[places + 4 :]
     _, me_place, me_core = layout.here()
     rows = places * samples
+    key_rows = len(keys) * samples
     group = min(GROUP_ROWS, rows)
     blocks = group // samples
     near = CORES * samples
+    for place, ref in enumerate(queries):
+        stage(ref, query_parts, place * samples, rows, samples, chunks)
     for place, ref in enumerate(keys):
-        stage(ref, key_parts, place * samples, samples, chunks)
-    for place, ref in enumerate(queries):
-        stage(ref, query_parts, place * samples, samples, chunks)
-    key_tail = tail_rows(keys, samples, chunks)
-    key_sign, key_norm = key_tail[0:1, :], key_tail[1:2, :]
-    tail_ref[...] = jnp.transpose(tail_rows(queries, samples, chunks))
+        stage(ref, key_parts, place * samples, key_rows, samples, chunks)
+    key_tail = as_columns(tail_rows(keys, samples, chunks))
+    key_sign, key_norm = key_tail[:, 0:1], key_tail[:, 1:2]
+    tail_ref[...] = tail_rows(queries, samples, chunks)
     lane = lax.broadcasted_iota(jnp.int32, (samples, LANES), 1)
 
     def one_group(index, carry):
         result, total, column = carry
         start = pl.multiple_of(index * group, group)
-        high, mid = (part[pl.ds(start, group), :] for part in query_parts)
-        key_high, key_mid = (part[...] for part in key_parts)
-        inner = bf16_dot(mid, key_mid, NT_DIMS)
-        inner = inner + (bf16_dot(high, key_mid, NT_DIMS) + bf16_dot(mid, key_high, NT_DIMS))
-        inner = inner + bf16_dot(high, key_high, NT_DIMS)
-        sign = tail_ref[pl.ds(start, group), 0:1]
-        norm = tail_ref[pl.ds(start, group), 1:2]
+        both = key_parts[...]
+        by_high = bf16_dot(both, query_parts[pl.ds(start, group), :], NT_DIMS)
+        by_mid = bf16_dot(both, query_parts[pl.ds(rows + start, group), :], NT_DIMS)
+        inner = by_high[:key_rows] + (by_high[key_rows:] + by_mid[:key_rows] + by_mid[key_rows:])
+        sign = tail_ref[0:1, pl.ds(start, group)]
+        norm = tail_ref[1:2, pl.ds(start, group)]
         sq_dist = norm + key_norm - 2.0 * inner
         kernel = jnp.exp(sq_dist * (-1.0 / 200.0))
         signed = kernel * key_sign
-        near_sums = jnp.sum(signed[:, :near], axis=1, keepdims=True)
-        far_sums = jnp.sum(signed[:, near:], axis=1, keepdims=True)
+        near_sums = jnp.sum(signed[:near], axis=0, keepdims=True)
+        far_sums = jnp.sum(signed[near:], axis=0, keepdims=True)
         sums = near_sums + far_sums
-        total = total + jnp.sum(sign * (sums + far_sums), axis=0, keepdims=True)
-        column = column + jnp.sum(kernel[:, near:] * sign, axis=0, keepdims=True)
+        total = total + jnp.sum(sign * (sums + far_sums), axis=1, keepdims=True)
+        column = column + jnp.sum(kernel[near:] * sign, axis=1, keepdims=True)
+        sums = as_columns(jnp.broadcast_to(sums, (SUBLANES, group)))
         for place in range(blocks):
             owner = me_place ^ (index * blocks + place)
             result = jnp.where(
-                lane == owner, sums[place * samples : (place + 1) * samples, :], result
+                lane == owner, sums[place * samples : (place + 1) * samples, 0:1], result
             )
         return result, total, column
 
     carry = (
         jnp.zeros((samples, LANES), jnp.float32),
         jnp.zeros((1, 1), jnp.float32),
-        jnp.zeros((1, FAR_BLOCKS * samples), jnp.float32),
+        jnp.zeros((FAR_BLOCKS * samples, 1), jnp.float32),
     )
     if rows == group:
         carry = one_group(0, carry)
     else:
         carry = lax.fori_loop(0, rows // group, one_group, carry)
     result, total, column = carry
-    column = jnp.concatenate([column, jnp.zeros((1, samples), jnp.float32)], axis=1)
-    column = jnp.transpose(jnp.broadcast_to(column, (SUBLANES, (FAR_BLOCKS + 1) * samples)))
     for place, offset in enumerate((me_core, 1 - me_core, 2)):
         result = jnp.where(
-            lane == places + offset, column[place * samples : (place + 1) * samples, 0:1], result
+            lane == places + offset, column[place * samples : (place + 1) * samples], result
         )
     out_ref[...] = jnp.where(lane == places + 4, total, result)
 
@@ -306,9 +310,11 @@
         out_shape=pltpu.VMEM((samples, LANES), jnp.float32),
         in_specs=vmem_specs(len(blocks)),
         out_specs=pl.BlockSpec(memory_space=pltpu.VMEM),
-        scratch_shapes=[pltpu.VMEM((key_rows, width), jnp.bfloat16)] * 2
-        + [pltpu.VMEM((query_rows, width), jnp.bfloat16)] * 2
-        + [pltpu.VMEM((query_rows, SUBLANES), jnp.float32)],
+        scratch_shapes=[
+            pltpu.VMEM((2 * key_rows, width), jnp.bfloat16),
+            pltpu.VMEM((2 * query_rows, width), jnp.bfloat16),
+            pltpu.VMEM((SUBLANES, query_rows), jnp.float32),
+        ],
         compiler_params=params,
         name="kernel_sums",
     )(*[in_vmem(block) for block in blocks])

time: 30.5 us -> 30.2 us (level)
  Pallas kernels: 3.37 us -> 3.06 us
    pallas_call x1, Pallas kernels: 1.32 us -> 1.01 us  [local(): pl.pallas_call(functools.partial(main_kernel, samples, chunks, layout), o...]
where the time goes in v2:
time: 30.2 us; the launch traced here: 30 us
  blocking collectives  9.29 us (31%)
  starting transfers between devices  9.06 us (30%)
  waiting for transfers between devices  7.93 us (26%)
  Pallas kernels  3.06 us (10%)
  between operations  0.66 us (2%)
    all_to_all x1, blocking collectives, local(): lax.all_to_all(partial, ('row', 'col'), split_axis=0, concat_axis=0, tile...  9.29 us
    ppermute x7, starting transfers between devices, send(): return lax.ppermute(block, ('row', 'col'), layout.pairs(target))  9.06 us
    ppermute x7, waiting for transfers between devices, send(): return lax.ppermute(block, ('row', 'col'), layout.pairs(target))  7.93 us
    pallas_call x1, Pallas kernels, local(): pl.pallas_call(pack_kernel, out_shape=(pltpu.VMEM((pack_rows, LANES), jnp...  1.21 us
    pallas_call x1, Pallas kernels, local(): pl.pallas_call(functools.partial(main_kernel, samples, chunks, layout), o...  1.01 us
    pallas_call x1, Pallas kernels, local(): pl.pallas_call(functools.partial(last_kernel, layout, samples, per_peer,...  0.84 us
  transfers between devices with their start and end apart: 7, of which 3 were waited for; matrix products, arithmetic and copies ran while one was open for 0% of the time, Pallas kernels for 0%

profile of v2, /device:TPU:0, one launch (start us, length us, event | category | flops | bytes accessed | tf_op | source)
XLA Modules:
  0.0 30.0 jit_solution(5248080187287557985)
XLA Ops:
  0.6 1.2 %pack_block.1 = (f32[392,128]{1,0:T(8,128)S(1)}, s32[1,64]{1,0:T(1,128)S(1)}) custom-call(f32[64,768]{1,0:T(8,128)} %emb_ref.1, s32[1,64]{1,0:T(1,128)} %bitcast.8, s32[1,64]{1,0:T(1,128)} %bitcast.9), custom_call_target="tpu_custom_call" | custom-call | tf_op jit(solution)/shard_map/pack_block/pallas_call | solution.py:269
  1.8 5.1 %collective-permute-start.3 = (f32[392,128]{1,0:T(8,128)S(1)}, f32[392,128]{1,0:T(8,128)S(1)}, u32[]{:S(2)}, u32[]{:S(2)}) collective-permute-start(f32[392,128]{1,0:T(8,128)S(1)} %get-tuple-element.8.refs_0_), channel_id=1, source_target_pairs={{0,24},{1,25},{2,26},{3,27},{4,28},{5,29},{6,30},{7,31},{8,16},{9,... | collective-permute-start | bytes 602120 | tf_op jit(solution)/shard_map/ppermute | solution.py:286
  6.9 2.4 %collective-permute-start.2 = (f32[392,128]{1,0:T(8,128)S(1)}, f32[392,128]{1,0:T(8,128)S(1)}, u32[]{:S(2)}, u32[]{:S(2)}) collective-permute-start(f32[392,128]{1,0:T(8,128)S(1)} %get-tuple-element.8.refs_0_), channel_id=1, source_target_pairs={{0,6},{1,7},{2,4},{3,5},{4,2},{5,3},{6,0},{7,1},{8,14},{9,15},{10,... | collective-permute-start | bytes 602120 | tf_op jit(solution)/shard_map/ppermute | solution.py:286
  9.4 0.0 collective-permute-start.6
  9.4 0.5 %collective-permute-start.1 = (f32[392,128]{1,0:T(8,128)S(1)}, f32[392,128]{1,0:T(8,128)S(1)}, u32[]{:S(2)}, u32[]{:S(2)}) collective-permute-start(f32[392,128]{1,0:T(8,128)S(1)} %get-tuple-element.8.refs_0_), channel_id=1, source_target_pairs={{0,4},{1,5},{2,6},{3,7},{4,0},{5,1},{6,2},{7,3},{8,12},{9,13},{10,... | collective-permute-start | bytes 602120 | tf_op jit(solution)/shard_map/ppermute | solution.py:286
  9.9 0.5 %collective-permute-start = (f32[392,128]{1,0:T(8,128)S(1)}, f32[392,128]{1,0:T(8,128)S(1)}, u32[]{:S(2)}, u32[]{:S(2)}) collective-permute-start(f32[392,128]{1,0:T(8,128)S(1)} %get-tuple-element.8.refs_0_), channel_id=1, source_target_pairs={{0,2},{1,3},{2,0},{3,1},{4,6},{5,7},{6,4},{7,5},{8,10},{9,11},{10,... | collective-permute-start | bytes 602120 | tf_op jit(solution)/shard_map/ppermute | solution.py:286
  10.4 4.9 %collective-permute-done.3.refs_5_ = f32[392,128]{1,0:T(8,128)S(1)} collective-permute-done((f32[392,128]{1,0:T(8,128)S(1)}, f32[392,128]{1,0:T(8,128)S(1)}, u32[]{:S(2)}, u32[]{:S(2)}) %collective-permute-start.3) | collective-permute-done | bytes 200736 | tf_op jit(solution)/shard_map/ppermute | solution.py:286
  15.3 0.4 %collective-permute-done.2.refs_3_ = f32[392,128]{1,0:T(8,128)S(1)} collective-permute-done((f32[392,128]{1,0:T(8,128)S(1)}, f32[392,128]{1,0:T(8,128)S(1)}, u32[]{:S(2)}, u32[]{:S(2)}) %collective-permute-start.2) | collective-permute-done | bytes 200736 | tf_op jit(solution)/shard_map/ppermute | solution.py:286
  15.7 0.0 collective-permute-start.5
  15.7 0.5 %collective-permute-start.4 = (f32[392,128]{1,0:T(8,128)S(1)}, f32[392,128]{1,0:T(8,128)S(1)}, u32[]{:S(2)}, u32[]{:S(2)}) collective-permute-start(f32[392,128]{1,0:T(8,128)S(1)} %get-tuple-element.8.refs_0_), channel_id=1, source_target_pairs={{0,1},{1,0},{2,3},{3,2},{4,5},{5,4},{6,7},{7,6},{8,9},{9,8},{10,11... | collective-permute-start | bytes 602120 | tf_op jit(solution)/shard_map/ppermute | solution.py:286
  16.2 2.6 %collective-permute-done.6.refs_7_ = f32[392,128]{1,0:T(8,128)S(1)} collective-permute-done((f32[392,128]{1,0:T(8,128)S(1)}, f32[392,128]{1,0:T(8,128)S(1)}, u32[]{:S(2)}, u32[]{:S(2)}) %collective-permute-start.6) | collective-permute-done | bytes 200736 | tf_op jit(solution)/shard_map/ppermute | solution.py:286
  18.8 0.0 collective-permute-done.1.refs_2_
  18.8 0.0 collective-permute-done.refs_1_
  18.8 0.0 collective-permute-done.5.refs_6_
  18.8 0.0 collective-permute-done.4.refs_4_
  18.9 1.0 %kernel_sums.1 = f32[64,128]{1,0:T(8,128)S(1)} custom-call(f32[392,128]{1,0:T(8,128)S(1)} %get-tuple-element.8.refs_0_, f32[392,128]{1,0:T(8,128)S(1)} %collective-permute-done.refs_1_, f32[392,128]{1,0:T(8,128)S(1)} %collective-permute-done.1.refs_2_, f32[392,128]{1,0:T(8,128)S(1)} %collective-permute-done.2.refs_3_, ...), custom_call_target="tpu_custom_call" | custom-call | tf_op jit(solution)/shard_map/kernel_sums/pallas_call | solution.py:308
  19.9 9.3 %all_to_all.11 = f32[32,2,128]{2,1,0:T(2,128)S(1)} all-to-all(f32[32,2,128]{2,1,0:T(2,128)S(1)} %bitcast.6), channel_id=1, replica_groups=mesh['row'=4,'col'=8] {'row','col'}, dimensions={0} | all-to-all | bytes 65536 | tf_op jit(solution)/shard_map/all_to_all | solution.py:322
  29.2 0.8 %pick_proof.1 = (f32[1,64]{1,0:T(1,128)}, f32[1,1]{1,0:T(1,128)}) custom-call(f32[64,128]{1,0:T(8,128)S(1)} %bitcast.7, s32[1,64]{1,0:T(1,128)S(1)} %get-tuple-element.9.id_ref), custom_call_target="tpu_custom_call" | custom-call | tf_op jit(solution)/shard_map/pick_proof/pallas_call | solution.py:324
Async XLA Ops:
  1.8 13.4 %collective-permute-start.3 = (f32[392,128]{1,0:T(8,128)S(1)}, f32[392,128]{1,0:T(8,128)S(1)}, u32[]{:S(2)}, u32[]{:S(2)}) collective-permute-start(f32[392,128]{1,0:T(8,128)S(1)} %get-tuple-element.8.refs_0_), channel_id=1, source_target_pairs={{0,24},{1,25},{2,26},{3,27},{4,28},{5,29},{6,30},{7,31},{8,16},{9,... | collective-permute-start | bytes 602120 | tf_op jit(solution)/shard_map/ppermute | solution.py:286
  6.9 8.8 %collective-permute-start.2 = (f32[392,128]{1,0:T(8,128)S(1)}, f32[392,128]{1,0:T(8,128)S(1)}, u32[]{:S(2)}, u32[]{:S(2)}) collective-permute-start(f32[392,128]{1,0:T(8,128)S(1)} %get-tuple-element.8.refs_0_), channel_id=1, source_target_pairs={{0,6},{1,7},{2,4},{3,5},{4,2},{5,3},{6,0},{7,1},{8,14},{9,15},{10,... | collective-permute-start | bytes 602120 | tf_op jit(solution)/shard_map/ppermute | solution.py:286
  9.4 9.5 %collective-permute-start.6 = (f32[392,128]{1,0:T(8,128)S(1)}, f32[392,128]{1,0:T(8,128)S(1)}, u32[]{:S(2)}, u32[]{:S(2)}) collective-permute-start(f32[392,128]{1,0:T(8,128)S(1)} %get-tuple-element.8.refs_0_), channel_id=1, source_target_pairs={{0,8},{1,9},{2,10},{3,11},{4,12},{5,13},{6,14},{7,15},{8,1},{9,0},... | collective-permute-start | bytes 602120 | tf_op jit(solution)/shard_map/ppermute | solution.py:286
  9.4 9.5 %collective-permute-start.1 = (f32[392,128]{1,0:T(8,128)S(1)}, f32[392,128]{1,0:T(8,128)S(1)}, u32[]{:S(2)}, u32[]{:S(2)}) collective-permute-start(f32[392,128]{1,0:T(8,128)S(1)} %get-tuple-element.8.refs_0_), channel_id=1, source_target_pairs={{0,4},{1,5},{2,6},{3,7},{4,0},{5,1},{6,2},{7,3},{8,12},{9,13},{10,... | collective-permute-start | bytes 602120 | tf_op jit(solution)/shard_map/ppermute | solution.py:286
  9.9 9.0 %collective-permute-start = (f32[392,128]{1,0:T(8,128)S(1)}, f32[392,128]{1,0:T(8,128)S(1)}, u32[]{:S(2)}, u32[]{:S(2)}) collective-permute-start(f32[392,128]{1,0:T(8,128)S(1)} %get-tuple-element.8.refs_0_), channel_id=1, source_target_pairs={{0,2},{1,3},{2,0},{3,1},{4,6},{5,7},{6,4},{7,5},{8,10},{9,11},{10,... | collective-permute-start | bytes 602120 | tf_op jit(solution)/shard_map/ppermute | solution.py:286
  15.7 3.1 %collective-permute-start.5 = (f32[392,128]{1,0:T(8,128)S(1)}, f32[392,128]{1,0:T(8,128)S(1)}, u32[]{:S(2)}, u32[]{:S(2)}) collective-permute-start(f32[392,128]{1,0:T(8,128)S(1)} %collective-permute-done.3.refs_5_), channel_id=1, source_target_pairs={{0,1},{1,0},{2,3},{3,2},{4,5},{5,4},{6,7},{7,6},{8,9},{9,8},{10,11... | collective-permute-start | bytes 602120 | tf_op jit(solution)/shard_map/ppermute | solution.py:286
  15.7 3.1 %collective-permute-start.4 = (f32[392,128]{1,0:T(8,128)S(1)}, f32[392,128]{1,0:T(8,128)S(1)}, u32[]{:S(2)}, u32[]{:S(2)}) collective-permute-start(f32[392,128]{1,0:T(8,128)S(1)} %get-tuple-element.8.refs_0_), channel_id=1, source_target_pairs={{0,1},{1,0},{2,3},{3,2},{4,5},{5,4},{6,7},{7,6},{8,9},{9,8},{10,11... | collective-permute-start | bytes 602120 | tf_op jit(solution)/shard_map/ppermute | solution.py:286

commit v3 on v2

--- a/solution.py
+++ b/solution.py
@@ -297,14 +297,15 @@
     def to_core(plane, place, core):
         return (plane, place, 1 - core)
 
-    in_plane = [send(packed, to_place(step)) for step in range(1, places)]
     far_b = send(packed, round_b)
+    in_plane = [None] + [send(packed, to_place(step)) for step in range(1, places)]
     far_a = send(packed, round_a)
-    far_a_other = send(far_a, to_core)
-    late, *_ = lax.optimization_barrier((packed, in_plane[-1], far_a))
+    late_a, *_ = lax.optimization_barrier((far_a, in_plane[2], in_plane[1]))
+    far_a_other = send(late_a, to_core)
+    late, *_ = lax.optimization_barrier((packed, in_plane[2]))
     near = send(late, to_core)
 
-    blocks = [packed, *in_plane, near, far_a, far_a_other, far_b]
+    blocks = [packed, *in_plane[1:], near, far_a, far_a_other, far_b]
     partial = pl.pallas_call(
         functools.partial(main_kernel, samples, chunks, layout),
         out_shape=pltpu.VMEM((samples, LANES), jnp.float32),

time: 30.2 us -> 30.7 us (1.017)
  waiting for transfers between devices: 7.93 us -> 9.09 us
  starting transfers between devices: 9.06 us -> 8.56 us
    ppermute x7, waiting for transfers between devices: 7.93 us -> 9.09 us  [send(): return lax.ppermute(block, ('row', 'col'), layout.pairs(target))]
    ppermute x7, starting transfers between devices: 9.06 us -> 8.56 us  [send(): return lax.ppermute(block, ('row', 'col'), layout.pairs(target))]
  transfers between devices with their start and end apart: 7 -> 7, of which waited for: 3 -> 2; matrix products, arithmetic and copies ran while one was open for 0% -> 0% of each run, Pallas kernels for 0% -> 0%
where the time goes in v3:
time: 30.7 us; the launch traced here: 30.6 us
  blocking collectives  9.21 us (30%)
  waiting for transfers between devices  9.09 us (30%)
  starting transfers between devices  8.56 us (28%)
  Pallas kernels  3.05 us (10%)
  between operations  0.65 us (2%)
    all_to_all x1, blocking collectives, local(): lax.all_to_all(partial, ('row', 'col'), split_axis=0, concat_axis=0, tile...  9.21 us
    ppermute x7, waiting for transfers between devices, send(): return lax.ppermute(block, ('row', 'col'), layout.pairs(target))  9.09 us
    ppermute x7, starting transfers between devices, send(): return lax.ppermute(block, ('row', 'col'), layout.pairs(target))  8.56 us
    pallas_call x1, Pallas kernels, local(): pl.pallas_call(pack_kernel, out_shape=(pltpu.VMEM((pack_rows, LANES), jnp...  1.21 us
    pallas_call x1, Pallas kernels, local(): pl.pallas_call(functools.partial(main_kernel, samples, chunks, layout), o...  1 us
    pallas_call x1, Pallas kernels, local(): pl.pallas_call(functools.partial(last_kernel, layout, samples, per_peer,...  0.84 us
  transfers between devices with their start and end apart: 7, of which 2 were waited for; matrix products, arithmetic and copies ran while one was open for 0% of the time, Pallas kernels for 0%

profile of v3, /device:TPU:0, one launch (start us, length us, event | category | flops | bytes accessed | tf_op | source)
XLA Modules:
  0.0 30.6 jit_solution(702291339880794178)
XLA Ops:
  0.6 1.2 %pack_block.1 = (f32[392,128]{1,0:T(8,128)S(1)}, s32[1,64]{1,0:T(1,128)S(1)}) custom-call(f32[64,768]{1,0:T(8,128)} %emb_ref.1, s32[1,64]{1,0:T(1,128)} %bitcast.8, s32[1,64]{1,0:T(1,128)} %bitcast.9), custom_call_target="tpu_custom_call" | custom-call | tf_op jit(solution)/shard_map/pack_block/pallas_call | solution.py:269
  1.8 3.0 %collective-permute-start.1 = (f32[392,128]{1,0:T(8,128)S(1)}, f32[392,128]{1,0:T(8,128)S(1)}, u32[]{:S(2)}, u32[]{:S(2)}) collective-permute-start(f32[392,128]{1,0:T(8,128)S(1)} %get-tuple-element.9.refs_0_), channel_id=1, source_target_pairs={{0,4},{1,5},{2,6},{3,7},{4,0},{5,1},{6,2},{7,3},{8,12},{9,13},{10,... | collective-permute-start | bytes 602120 | tf_op jit(solution)/shard_map/ppermute | solution.py:286
  4.8 3.6 %collective-permute-start.4 = (f32[392,128]{1,0:T(8,128)S(1)}, f32[392,128]{1,0:T(8,128)S(1)}, u32[]{:S(2)}, u32[]{:S(2)}) collective-permute-start(f32[392,128]{1,0:T(8,128)S(1)} %get-tuple-element.9.refs_0_), channel_id=1, source_target_pairs={{0,24},{1,25},{2,26},{3,27},{4,28},{5,29},{6,30},{7,31},{8,16},{9,... | collective-permute-start | bytes 602120 | tf_op jit(solution)/shard_map/ppermute | solution.py:286
  8.4 1.5 %collective-permute-start = (f32[392,128]{1,0:T(8,128)S(1)}, f32[392,128]{1,0:T(8,128)S(1)}, u32[]{:S(2)}, u32[]{:S(2)}) collective-permute-start(f32[392,128]{1,0:T(8,128)S(1)} %get-tuple-element.9.refs_0_), channel_id=1, source_target_pairs={{0,2},{1,3},{2,0},{3,1},{4,6},{5,7},{6,4},{7,5},{8,10},{9,11},{10,... | collective-permute-start | bytes 602120 | tf_op jit(solution)/shard_map/ppermute | solution.py:286
  9.9 0.0 collective-permute-start.6
  9.9 0.5 %collective-permute-start.2 = (f32[392,128]{1,0:T(8,128)S(1)}, f32[392,128]{1,0:T(8,128)S(1)}, u32[]{:S(2)}, u32[]{:S(2)}) collective-permute-start(f32[392,128]{1,0:T(8,128)S(1)} %get-tuple-element.9.refs_0_), channel_id=1, source_target_pairs={{0,6},{1,7},{2,4},{3,5},{4,2},{5,3},{6,0},{7,1},{8,14},{9,15},{10,... | collective-permute-start | bytes 602120 | tf_op jit(solution)/shard_map/ppermute | solution.py:286
  10.4 0.0 collective-permute-done.1.refs_2_
  10.4 0.0 collective-permute-start.3
  10.4 6.2 %collective-permute-done.4.refs_5_ = f32[392,128]{1,0:T(8,128)S(1)} collective-permute-done((f32[392,128]{1,0:T(8,128)S(1)}, f32[392,128]{1,0:T(8,128)S(1)}, u32[]{:S(2)}, u32[]{:S(2)}) %collective-permute-start.4) | collective-permute-done | bytes 200736 | tf_op jit(solution)/shard_map/ppermute | solution.py:286
  16.6 0.0 collective-permute-done.refs_1_
  16.6 0.0 collective-permute-start.5
  16.6 2.9 %collective-permute-done.6.refs_7_ = f32[392,128]{1,0:T(8,128)S(1)} collective-permute-done((f32[392,128]{1,0:T(8,128)S(1)}, f32[392,128]{1,0:T(8,128)S(1)}, u32[]{:S(2)}, u32[]{:S(2)}) %collective-permute-start.6) | collective-permute-done | bytes 200736 | tf_op jit(solution)/shard_map/ppermute | solution.py:286
  19.5 0.0 collective-permute-done.2.refs_3_
  19.5 0.0 collective-permute-done.3.refs_4_
  19.5 0.0 collective-permute-done.5.refs_6_
  19.5 1.0 %kernel_sums.1 = f32[64,128]{1,0:T(8,128)S(1)} custom-call(f32[392,128]{1,0:T(8,128)S(1)} %get-tuple-element.9.refs_0_, f32[392,128]{1,0:T(8,128)S(1)} %collective-permute-done.refs_1_, f32[392,128]{1,0:T(8,128)S(1)} %collective-permute-done.1.refs_2_, f32[392,128]{1,0:T(8,128)S(1)} %collective-permute-done.2.refs_3_, ...), custom_call_target="tpu_custom_call" | custom-call | tf_op jit(solution)/shard_map/kernel_sums/pallas_call | solution.py:309
  20.5 9.2 %all_to_all.11 = f32[32,2,128]{2,1,0:T(2,128)S(1)} all-to-all(f32[32,2,128]{2,1,0:T(2,128)S(1)} %bitcast.6), channel_id=1, replica_groups=mesh['row'=4,'col'=8] {'row','col'}, dimensions={0} | all-to-all | bytes 65536 | tf_op jit(solution)/shard_map/all_to_all | solution.py:323
  29.7 0.8 %pick_proof.1 = (f32[1,64]{1,0:T(1,128)}, f32[1,1]{1,0:T(1,128)}) custom-call(f32[64,128]{1,0:T(8,128)S(1)} %bitcast.7, s32[1,64]{1,0:T(1,128)S(1)} %get-tuple-element.11.id_ref), custom_call_target="tpu_custom_call" | custom-call | tf_op jit(solution)/shard_map/pick_proof/pallas_call | solution.py:325
Async XLA Ops:
  1.8 8.6 %collective-permute-start.1 = (f32[392,128]{1,0:T(8,128)S(1)}, f32[392,128]{1,0:T(8,128)S(1)}, u32[]{:S(2)}, u32[]{:S(2)}) collective-permute-start(f32[392,128]{1,0:T(8,128)S(1)} %get-tuple-element.9.refs_0_), channel_id=1, source_target_pairs={{0,4},{1,5},{2,6},{3,7},{4,0},{5,1},{6,2},{7,3},{8,12},{9,13},{10,... | collective-permute-start | bytes 602120 | tf_op jit(solution)/shard_map/ppermute | solution.py:286
  4.8 11.8 %collective-permute-start.4 = (f32[392,128]{1,0:T(8,128)S(1)}, f32[392,128]{1,0:T(8,128)S(1)}, u32[]{:S(2)}, u32[]{:S(2)}) collective-permute-start(f32[392,128]{1,0:T(8,128)S(1)} %get-tuple-element.9.refs_0_), channel_id=1, source_target_pairs={{0,24},{1,25},{2,26},{3,27},{4,28},{5,29},{6,30},{7,31},{8,16},{9,... | collective-permute-start | bytes 602120 | tf_op jit(solution)/shard_map/ppermute | solution.py:286
  8.4 8.2 %collective-permute-start = (f32[392,128]{1,0:T(8,128)S(1)}, f32[392,128]{1,0:T(8,128)S(1)}, u32[]{:S(2)}, u32[]{:S(2)}) collective-permute-start(f32[392,128]{1,0:T(8,128)S(1)} %get-tuple-element.9.refs_0_), channel_id=1, source_target_pairs={{0,2},{1,3},{2,0},{3,1},{4,6},{5,7},{6,4},{7,5},{8,10},{9,11},{10,... | collective-permute-start | bytes 602120 | tf_op jit(solution)/shard_map/ppermute | solution.py:286
  9.9 9.6 %collective-permute-start.6 = (f32[392,128]{1,0:T(8,128)S(1)}, f32[392,128]{1,0:T(8,128)S(1)}, u32[]{:S(2)}, u32[]{:S(2)}) collective-permute-start(f32[392,128]{1,0:T(8,128)S(1)} %get-tuple-element.9.refs_0_), channel_id=1, source_target_pairs={{0,8},{1,9},{2,10},{3,11},{4,12},{5,13},{6,14},{7,15},{8,1},{9,0},... | collective-permute-start | bytes 602120 | tf_op jit(solution)/shard_map/ppermute | solution.py:286
  9.9 9.6 %collective-permute-start.2 = (f32[392,128]{1,0:T(8,128)S(1)}, f32[392,128]{1,0:T(8,128)S(1)}, u32[]{:S(2)}, u32[]{:S(2)}) collective-permute-start(f32[392,128]{1,0:T(8,128)S(1)} %get-tuple-element.9.refs_0_), channel_id=1, source_target_pairs={{0,6},{1,7},{2,4},{3,5},{4,2},{5,3},{6,0},{7,1},{8,14},{9,15},{10,... | collective-permute-start | bytes 602120 | tf_op jit(solution)/shard_map/ppermute | solution.py:286
  10.4 9.1 %collective-permute-start.3 = (f32[392,128]{1,0:T(8,128)S(1)}, f32[392,128]{1,0:T(8,128)S(1)}, u32[]{:S(2)}, u32[]{:S(2)}) collective-permute-start(f32[392,128]{1,0:T(8,128)S(1)} %get-tuple-element.9.refs_0_), channel_id=1, source_target_pairs={{0,1},{1,0},{2,3},{3,2},{4,5},{5,4},{6,7},{7,6},{8,9},{9,8},{10,11... | collective-permute-start | bytes 602120 | tf_op jit(solution)/shard_map/ppermute | solution.py:286
  16.6 2.9 %collective-permute-start.5 = (f32[392,128]{1,0:T(8,128)S(1)}, f32[392,128]{1,0:T(8,128)S(1)}, u32[]{:S(2)}, u32[]{:S(2)}) collective-permute-start(f32[392,128]{1,0:T(8,128)S(1)} %collective-permute-done.4.refs_5_), channel_id=1, source_target_pairs={{0,1},{1,0},{2,3},{3,2},{4,5},{5,4},{6,7},{7,6},{8,9},{9,8},{10,11... | collective-permute-start | bytes 602120 | tf_op jit(solution)/shard_map/ppermute | solution.py:286

commit v4 on v2

--- a/solution.py
+++ b/solution.py
@@ -84,21 +84,32 @@
     return lax.dot_general(left, right, dims, preferred_element_type=jnp.float32)
 
 
-def pack_kernel(emb_ref, label_ref, id_ref, out_ref, id_out_ref):
+def pack_kernel(emb_ref, label_ref, id_ref, out_ref, id_out_ref, label_vmem, copied):
     samples, width = emb_ref.shape
-    id_out_ref[...] = id_ref[...]
-    emb = emb_ref[...]
-    norm = lax.dot_general(
-        jnp.ones((SUBLANES, width), jnp.float32),
-        emb * emb,
-        NT_DIMS,
-        precision=lax.Precision.HIGHEST,
-        preferred_element_type=jnp.float32,
-    )
-    sign = (1 - 2 * label_ref[...]).astype(jnp.float32)
-    for chunk in range(width // LANES):
-        out_ref[pl.ds(chunk * samples, samples), :] = emb[:, chunk * LANES : (chunk + 1) * LANES]
-    base = samples * (width // LANES)
+    chunks = width // LANES
+    copies = [
+        pltpu.make_async_copy(
+            emb_ref.at[:, pl.ds(chunk * LANES, LANES)],
+            out_ref.at[pl.ds(chunk * samples, samples), :],
+            copied.at[chunk],
+        )
+        for chunk in range(chunks)
+    ]
+    copies.append(pltpu.make_async_copy(label_ref, label_vmem, copied.at[chunks]))
+    copies.append(pltpu.make_async_copy(id_ref, id_out_ref, copied.at[chunks + 1]))
+    for copy in copies:
+        copy.start()
+    squares = jnp.zeros((samples, LANES), jnp.float32)
+    for chunk in range(chunks):
+        copies[chunk].wait()
+        value = out_ref[pl.ds(chunk * samples, samples), :]
+        squares = squares + value * value
+    ones = jnp.ones((SUBLANES, LANES), jnp.bfloat16)
+    high, mid, low = (bf16_dot(ones, part, NT_DIMS) for part in split3(squares))
+    norm = high + (mid + low)
+    copies[chunks].wait()
+    sign = (1 - 2 * label_vmem[...]).astype(jnp.float32)
+    base = samples * chunks
     row = lax.broadcasted_iota(jnp.int32, (SUBLANES, samples), 0)
     both = jnp.where(row == 0, sign, norm)
     for start in range(0, samples, LANES):
@@ -107,6 +118,7 @@
         if lanes < LANES:
             out_ref[pl.ds(place, SUBLANES), :] = jnp.zeros((SUBLANES, LANES), jnp.float32)
         out_ref[pl.ds(place, SUBLANES), pl.ds(0, lanes)] = both[:, start : start + lanes]
+    copies[chunks + 1].wait()
 
 
 def stage(ref, scratch, start, middle, samples, chunks):
@@ -272,8 +284,12 @@
             pltpu.VMEM((pack_rows, LANES), jnp.float32),
             pltpu.VMEM((1, samples), jnp.int32),
         ),
-        in_specs=vmem_specs(3),
+        in_specs=[pl.BlockSpec(memory_space=pl.ANY)] * 3,
         out_specs=tuple(vmem_specs(2)),
+        scratch_shapes=[
+            pltpu.VMEM((1, samples), jnp.int32),
+            pltpu.SemaphoreType.DMA((chunks + 2,)),
+        ],
         compiler_params=pltpu.CompilerParams(vmem_limit_bytes=4 * block_bytes + 4 * MIB),
         name="pack_block",
     )(

time: 30.2 us -> 30.1 us (level)
  no operation moved by 1% of the time
where the time goes in v4:
time: 30.1 us; the launch traced here: 29.9 us
  blocking collectives  9.31 us (31%)
  starting transfers between devices  9.1 us (30%)
  waiting for transfers between devices  7.93 us (26%)
  Pallas kernels  2.92 us (10%)
  between operations  0.66 us (2%)
    all_to_all x1, blocking collectives, local(): lax.all_to_all(partial, ('row', 'col'), split_axis=0, concat_axis=0, tile...  9.31 us
    ppermute x7, starting transfers between devices, send(): return lax.ppermute(block, ('row', 'col'), layout.pairs(target))  9.1 us
    ppermute x7, waiting for transfers between devices, send(): return lax.ppermute(block, ('row', 'col'), layout.pairs(target))  7.93 us
    pallas_call x1, Pallas kernels, local(): pl.pallas_call(pack_kernel, out_shape=(pltpu.VMEM((pack_rows, LANES), jnp...  1.07 us
    pallas_call x1, Pallas kernels, local(): pl.pallas_call(functools.partial(main_kernel, samples, chunks, layout), o...  1.01 us
    pallas_call x1, Pallas kernels, local(): pl.pallas_call(functools.partial(last_kernel, layout, samples, per_peer,...  0.84 us
  transfers between devices with their start and end apart: 7, of which 3 were waited for; matrix products, arithmetic and copies ran while one was open for 0% of the time, Pallas kernels for 0%

profile of v4, /device:TPU:0, one launch (start us, length us, event | category | flops | bytes accessed | tf_op | source)
XLA Modules:
  0.0 29.9 jit_solution(6236890531125713274)
XLA Ops:
  0.6 1.1 %pack_block.1 = (f32[392,128]{1,0:T(8,128)S(1)}, s32[1,64]{1,0:T(1,128)S(1)}) custom-call(f32[64,768]{1,0:T(8,128)} %emb_ref.1, s32[1,64]{1,0:T(1,128)} %bitcast.8, s32[1,64]{1,0:T(1,128)} %bitcast.9), custom_call_target="tpu_custom_call" | custom-call | tf_op jit(solution)/shard_map/pack_block/pallas_call | solution.py:281
  1.7 5.1 %collective-permute-start.3 = (f32[392,128]{1,0:T(8,128)S(1)}, f32[392,128]{1,0:T(8,128)S(1)}, u32[]{:S(2)}, u32[]{:S(2)}) collective-permute-start(f32[392,128]{1,0:T(8,128)S(1)} %get-tuple-element.8.refs_0_), channel_id=1, source_target_pairs={{0,24},{1,25},{2,26},{3,27},{4,28},{5,29},{6,30},{7,31},{8,16},{9,... | collective-permute-start | bytes 602120 | tf_op jit(solution)/shard_map/ppermute | solution.py:302
  6.8 2.4 %collective-permute-start.2 = (f32[392,128]{1,0:T(8,128)S(1)}, f32[392,128]{1,0:T(8,128)S(1)}, u32[]{:S(2)}, u32[]{:S(2)}) collective-permute-start(f32[392,128]{1,0:T(8,128)S(1)} %get-tuple-element.8.refs_0_), channel_id=1, source_target_pairs={{0,6},{1,7},{2,4},{3,5},{4,2},{5,3},{6,0},{7,1},{8,14},{9,15},{10,... | collective-permute-start | bytes 602120 | tf_op jit(solution)/shard_map/ppermute | solution.py:302
  9.3 0.0 collective-permute-start.6
  9.3 0.5 %collective-permute-start.1 = (f32[392,128]{1,0:T(8,128)S(1)}, f32[392,128]{1,0:T(8,128)S(1)}, u32[]{:S(2)}, u32[]{:S(2)}) collective-permute-start(f32[392,128]{1,0:T(8,128)S(1)} %get-tuple-element.8.refs_0_), channel_id=1, source_target_pairs={{0,4},{1,5},{2,6},{3,7},{4,0},{5,1},{6,2},{7,3},{8,12},{9,13},{10,... | collective-permute-start | bytes 602120 | tf_op jit(solution)/shard_map/ppermute | solution.py:302
  9.8 0.5 %collective-permute-start = (f32[392,128]{1,0:T(8,128)S(1)}, f32[392,128]{1,0:T(8,128)S(1)}, u32[]{:S(2)}, u32[]{:S(2)}) collective-permute-start(f32[392,128]{1,0:T(8,128)S(1)} %get-tuple-element.8.refs_0_), channel_id=1, source_target_pairs={{0,2},{1,3},{2,0},{3,1},{4,6},{5,7},{6,4},{7,5},{8,10},{9,11},{10,... | collective-permute-start | bytes 602120 | tf_op jit(solution)/shard_map/ppermute | solution.py:302
  10.3 4.9 %collective-permute-done.3.refs_5_ = f32[392,128]{1,0:T(8,128)S(1)} collective-permute-done((f32[392,128]{1,0:T(8,128)S(1)}, f32[392,128]{1,0:T(8,128)S(1)}, u32[]{:S(2)}, u32[]{:S(2)}) %collective-permute-start.3) | collective-permute-done | bytes 200736 | tf_op jit(solution)/shard_map/ppermute | solution.py:302
  15.2 0.4 %collective-permute-done.2.refs_3_ = f32[392,128]{1,0:T(8,128)S(1)} collective-permute-done((f32[392,128]{1,0:T(8,128)S(1)}, f32[392,128]{1,0:T(8,128)S(1)}, u32[]{:S(2)}, u32[]{:S(2)}) %collective-permute-start.2) | collective-permute-done | bytes 200736 | tf_op jit(solution)/shard_map/ppermute | solution.py:302
  15.6 0.0 collective-permute-start.5
  15.6 0.5 %collective-permute-start.4 = (f32[392,128]{1,0:T(8,128)S(1)}, f32[392,128]{1,0:T(8,128)S(1)}, u32[]{:S(2)}, u32[]{:S(2)}) collective-permute-start(f32[392,128]{1,0:T(8,128)S(1)} %get-tuple-element.8.refs_0_), channel_id=1, source_target_pairs={{0,1},{1,0},{2,3},{3,2},{4,5},{5,4},{6,7},{7,6},{8,9},{9,8},{10,11... | collective-permute-start | bytes 602120 | tf_op jit(solution)/shard_map/ppermute | solution.py:302
  16.1 2.6 %collective-permute-done.6.refs_7_ = f32[392,128]{1,0:T(8,128)S(1)} collective-permute-done((f32[392,128]{1,0:T(8,128)S(1)}, f32[392,128]{1,0:T(8,128)S(1)}, u32[]{:S(2)}, u32[]{:S(2)}) %collective-permute-start.6) | collective-permute-done | bytes 200736 | tf_op jit(solution)/shard_map/ppermute | solution.py:302
  18.7 0.0 collective-permute-done.1.refs_2_
  18.7 0.0 collective-permute-done.refs_1_
  18.7 0.0 collective-permute-done.5.refs_6_
  18.8 0.0 collective-permute-done.4.refs_4_
  18.8 1.0 %kernel_sums.1 = f32[64,128]{1,0:T(8,128)S(1)} custom-call(f32[392,128]{1,0:T(8,128)S(1)} %get-tuple-element.8.refs_0_, f32[392,128]{1,0:T(8,128)S(1)} %collective-permute-done.refs_1_, f32[392,128]{1,0:T(8,128)S(1)} %collective-permute-done.1.refs_2_, f32[392,128]{1,0:T(8,128)S(1)} %collective-permute-done.2.refs_3_, ...), custom_call_target="tpu_custom_call" | custom-call | tf_op jit(solution)/shard_map/kernel_sums/pallas_call | solution.py:324
  19.8 9.3 %all_to_all.11 = f32[32,2,128]{2,1,0:T(2,128)S(1)} all-to-all(f32[32,2,128]{2,1,0:T(2,128)S(1)} %bitcast.6), channel_id=1, replica_groups=mesh['row'=4,'col'=8] {'row','col'}, dimensions={0} | all-to-all | bytes 65536 | tf_op jit(solution)/shard_map/all_to_all | solution.py:338
  29.1 0.8 %pick_proof.1 = (f32[1,64]{1,0:T(1,128)}, f32[1,1]{1,0:T(1,128)}) custom-call(f32[64,128]{1,0:T(8,128)S(1)} %bitcast.7, s32[1,64]{1,0:T(1,128)S(1)} %get-tuple-element.9.id_ref), custom_call_target="tpu_custom_call" | custom-call | tf_op jit(solution)/shard_map/pick_proof/pallas_call | solution.py:340
Async XLA Ops:
  1.7 13.5 %collective-permute-start.3 = (f32[392,128]{1,0:T(8,128)S(1)}, f32[392,128]{1,0:T(8,128)S(1)}, u32[]{:S(2)}, u32[]{:S(2)}) collective-permute-start(f32[392,128]{1,0:T(8,128)S(1)} %get-tuple-element.8.refs_0_), channel_id=1, source_target_pairs={{0,24},{1,25},{2,26},{3,27},{4,28},{5,29},{6,30},{7,31},{8,16},{9,... | collective-permute-start | bytes 602120 | tf_op jit(solution)/shard_map/ppermute | solution.py:302
  6.8 8.8 %collective-permute-start.2 = (f32[392,128]{1,0:T(8,128)S(1)}, f32[392,128]{1,0:T(8,128)S(1)}, u32[]{:S(2)}, u32[]{:S(2)}) collective-permute-start(f32[392,128]{1,0:T(8,128)S(1)} %get-tuple-element.8.refs_0_), channel_id=1, source_target_pairs={{0,6},{1,7},{2,4},{3,5},{4,2},{5,3},{6,0},{7,1},{8,14},{9,15},{10,... | collective-permute-start | bytes 602120 | tf_op jit(solution)/shard_map/ppermute | solution.py:302
  9.3 9.5 %collective-permute-start.6 = (f32[392,128]{1,0:T(8,128)S(1)}, f32[392,128]{1,0:T(8,128)S(1)}, u32[]{:S(2)}, u32[]{:S(2)}) collective-permute-start(f32[392,128]{1,0:T(8,128)S(1)} %get-tuple-element.8.refs_0_), channel_id=1, source_target_pairs={{0,8},{1,9},{2,10},{3,11},{4,12},{5,13},{6,14},{7,15},{8,1},{9,0},... | collective-permute-start | bytes 602120 | tf_op jit(solution)/shard_map/ppermute | solution.py:302
  9.3 9.5 %collective-permute-start.1 = (f32[392,128]{1,0:T(8,128)S(1)}, f32[392,128]{1,0:T(8,128)S(1)}, u32[]{:S(2)}, u32[]{:S(2)}) collective-permute-start(f32[392,128]{1,0:T(8,128)S(1)} %get-tuple-element.8.refs_0_), channel_id=1, source_target_pairs={{0,4},{1,5},{2,6},{3,7},{4,0},{5,1},{6,2},{7,3},{8,12},{9,13},{10,... | collective-permute-start | bytes 602120 | tf_op jit(solution)/shard_map/ppermute | solution.py:302
  9.8 9.0 %collective-permute-start = (f32[392,128]{1,0:T(8,128)S(1)}, f32[392,128]{1,0:T(8,128)S(1)}, u32[]{:S(2)}, u32[]{:S(2)}) collective-permute-start(f32[392,128]{1,0:T(8,128)S(1)} %get-tuple-element.8.refs_0_), channel_id=1, source_target_pairs={{0,2},{1,3},{2,0},{3,1},{4,6},{5,7},{6,4},{7,5},{8,10},{9,11},{10,... | collective-permute-start | bytes 602120 | tf_op jit(solution)/shard_map/ppermute | solution.py:302
  15.6 3.1 %collective-permute-start.5 = (f32[392,128]{1,0:T(8,128)S(1)}, f32[392,128]{1,0:T(8,128)S(1)}, u32[]{:S(2)}, u32[]{:S(2)}) collective-permute-start(f32[392,128]{1,0:T(8,128)S(1)} %collective-permute-done.3.refs_5_), channel_id=1, source_target_pairs={{0,1},{1,0},{2,3},{3,2},{4,5},{5,4},{6,7},{7,6},{8,9},{9,8},{10,11... | collective-permute-start | bytes 602120 | tf_op jit(solution)/shard_map/ppermute | solution.py:302
  15.6 3.1 %collective-permute-start.4 = (f32[392,128]{1,0:T(8,128)S(1)}, f32[392,128]{1,0:T(8,128)S(1)}, u32[]{:S(2)}, u32[]{:S(2)}) collective-permute-start(f32[392,128]{1,0:T(8,128)S(1)} %get-tuple-element.8.refs_0_), channel_id=1, source_target_pairs={{0,1},{1,0},{2,3},{3,2},{4,5},{5,4},{6,7},{7,6},{8,9},{9,8},{10,11... | collective-permute-start | bytes 602120 | tf_op jit(solution)/shard_map/ppermute | solution.py:302

commit v5 on v4

--- a/solution.py
+++ b/solution.py
@@ -14,7 +14,7 @@
 CORES = 2
 ROUND_A = {2: 0, 3: 1, 1: 2, 0: 3}
 ROUND_B = {0: 1, 3: 2, 1: 0, 2: 3}
-CROSSING = (1, 2)
+CROSSING = (0, 3)
 FAR_BLOCKS = 3
 MIB = 1024 * 1024
 NT_DIMS = (((1,), (1,)), ((), ()))

time: 30.1 us -> 30.2 us (level)
  no operation moved by 1% of the time
where the time goes in v5:
time: 30.2 us; the launch traced here: 30 us
  blocking collectives  9.55 us (32%)
  starting transfers between devices  9.1 us (30%)
  waiting for transfers between devices  7.76 us (26%)
  Pallas kernels  2.92 us (10%)
  between operations  0.66 us (2%)
    all_to_all x1, blocking collectives, local(): lax.all_to_all(partial, ('row', 'col'), split_axis=0, concat_axis=0, tile...  9.55 us
    ppermute x7, starting transfers between devices, send(): return lax.ppermute(block, ('row', 'col'), layout.pairs(target))  9.1 us
    ppermute x7, waiting for transfers between devices, send(): return lax.ppermute(block, ('row', 'col'), layout.pairs(target))  7.76 us
    pallas_call x1, Pallas kernels, local(): pl.pallas_call(pack_kernel, out_shape=(pltpu.VMEM((pack_rows, LANES), jnp...  1.07 us
    pallas_call x1, Pallas kernels, local(): pl.pallas_call(functools.partial(main_kernel, samples, chunks, layout), o...  1.01 us
    pallas_call x1, Pallas kernels, local(): pl.pallas_call(functools.partial(last_kernel, layout, samples, per_peer,...  0.84 us
  transfers between devices with their start and end apart: 7, of which 3 were waited for; matrix products, arithmetic and copies ran while one was open for 0% of the time, Pallas kernels for 0%

profile of v5, /device:TPU:0, one launch (start us, length us, event | category | flops | bytes accessed | tf_op | source)
XLA Modules:
  0.0 30.0 jit_solution(15021875910567433791)
XLA Ops:
  0.6 1.1 %pack_block.1 = (f32[392,128]{1,0:T(8,128)S(1)}, s32[1,64]{1,0:T(1,128)S(1)}) custom-call(f32[64,768]{1,0:T(8,128)} %emb_ref.1, s32[1,64]{1,0:T(1,128)} %bitcast.8, s32[1,64]{1,0:T(1,128)} %bitcast.9), custom_call_target="tpu_custom_call" | custom-call | tf_op jit(solution)/shard_map/pack_block/pallas_call | solution.py:281
  1.7 5.1 %collective-permute-start.3 = (f32[392,128]{1,0:T(8,128)S(1)}, f32[392,128]{1,0:T(8,128)S(1)}, u32[]{:S(2)}, u32[]{:S(2)}) collective-permute-start(f32[392,128]{1,0:T(8,128)S(1)} %get-tuple-element.8.refs_0_), channel_id=1, source_target_pairs={{0,24},{1,25},{2,26},{3,27},{4,28},{5,29},{6,30},{7,31},{8,16},{9,... | collective-permute-start | bytes 602120 | tf_op jit(solution)/shard_map/ppermute | solution.py:302
  6.8 2.4 %collective-permute-start.2 = (f32[392,128]{1,0:T(8,128)S(1)}, f32[392,128]{1,0:T(8,128)S(1)}, u32[]{:S(2)}, u32[]{:S(2)}) collective-permute-start(f32[392,128]{1,0:T(8,128)S(1)} %get-tuple-element.8.refs_0_), channel_id=1, source_target_pairs={{0,6},{1,7},{2,4},{3,5},{4,2},{5,3},{6,0},{7,1},{8,14},{9,15},{10,... | collective-permute-start | bytes 602120 | tf_op jit(solution)/shard_map/ppermute | solution.py:302
  9.3 0.0 collective-permute-start.6
  9.3 0.5 %collective-permute-start.1 = (f32[392,128]{1,0:T(8,128)S(1)}, f32[392,128]{1,0:T(8,128)S(1)}, u32[]{:S(2)}, u32[]{:S(2)}) collective-permute-start(f32[392,128]{1,0:T(8,128)S(1)} %get-tuple-element.8.refs_0_), channel_id=1, source_target_pairs={{0,4},{1,5},{2,6},{3,7},{4,0},{5,1},{6,2},{7,3},{8,12},{9,13},{10,... | collective-permute-start | bytes 602120 | tf_op jit(solution)/shard_map/ppermute | solution.py:302
  9.8 0.5 %collective-permute-start = (f32[392,128]{1,0:T(8,128)S(1)}, f32[392,128]{1,0:T(8,128)S(1)}, u32[]{:S(2)}, u32[]{:S(2)}) collective-permute-start(f32[392,128]{1,0:T(8,128)S(1)} %get-tuple-element.8.refs_0_), channel_id=1, source_target_pairs={{0,2},{1,3},{2,0},{3,1},{4,6},{5,7},{6,4},{7,5},{8,10},{9,11},{10,... | collective-permute-start | bytes 602120 | tf_op jit(solution)/shard_map/ppermute | solution.py:302
  10.3 4.9 %collective-permute-done.3.refs_5_ = f32[392,128]{1,0:T(8,128)S(1)} collective-permute-done((f32[392,128]{1,0:T(8,128)S(1)}, f32[392,128]{1,0:T(8,128)S(1)}, u32[]{:S(2)}, u32[]{:S(2)}) %collective-permute-start.3) | collective-permute-done | bytes 200736 | tf_op jit(solution)/shard_map/ppermute | solution.py:302
  15.2 0.4 %collective-permute-done.2.refs_3_ = f32[392,128]{1,0:T(8,128)S(1)} collective-permute-done((f32[392,128]{1,0:T(8,128)S(1)}, f32[392,128]{1,0:T(8,128)S(1)}, u32[]{:S(2)}, u32[]{:S(2)}) %collective-permute-start.2) | collective-permute-done | bytes 200736 | tf_op jit(solution)/shard_map/ppermute | solution.py:302
  15.6 0.0 collective-permute-start.5
  15.6 0.5 %collective-permute-start.4 = (f32[392,128]{1,0:T(8,128)S(1)}, f32[392,128]{1,0:T(8,128)S(1)}, u32[]{:S(2)}, u32[]{:S(2)}) collective-permute-start(f32[392,128]{1,0:T(8,128)S(1)} %get-tuple-element.8.refs_0_), channel_id=1, source_target_pairs={{0,1},{1,0},{2,3},{3,2},{4,5},{5,4},{6,7},{7,6},{8,9},{9,8},{10,11... | collective-permute-start | bytes 602120 | tf_op jit(solution)/shard_map/ppermute | solution.py:302
  16.1 2.5 %collective-permute-done.6.refs_7_ = f32[392,128]{1,0:T(8,128)S(1)} collective-permute-done((f32[392,128]{1,0:T(8,128)S(1)}, f32[392,128]{1,0:T(8,128)S(1)}, u32[]{:S(2)}, u32[]{:S(2)}) %collective-permute-start.6) | collective-permute-done | bytes 200736 | tf_op jit(solution)/shard_map/ppermute | solution.py:302
  18.6 0.0 collective-permute-done.1.refs_2_
  18.6 0.0 collective-permute-done.refs_1_
  18.6 0.0 collective-permute-done.5.refs_6_
  18.6 0.0 collective-permute-done.4.refs_4_
  18.6 1.0 %kernel_sums.1 = f32[64,128]{1,0:T(8,128)S(1)} custom-call(f32[392,128]{1,0:T(8,128)S(1)} %get-tuple-element.8.refs_0_, f32[392,128]{1,0:T(8,128)S(1)} %collective-permute-done.refs_1_, f32[392,128]{1,0:T(8,128)S(1)} %collective-permute-done.1.refs_2_, f32[392,128]{1,0:T(8,128)S(1)} %collective-permute-done.2.refs_3_, ...), custom_call_target="tpu_custom_call" | custom-call | tf_op jit(solution)/shard_map/kernel_sums/pallas_call | solution.py:324
  19.6 9.5 %all_to_all.11 = f32[32,2,128]{2,1,0:T(2,128)S(1)} all-to-all(f32[32,2,128]{2,1,0:T(2,128)S(1)} %bitcast.6), channel_id=1, replica_groups=mesh['row'=4,'col'=8] {'row','col'}, dimensions={0} | all-to-all | bytes 65536 | tf_op jit(solution)/shard_map/all_to_all | solution.py:338
  29.2 0.8 %pick_proof.1 = (f32[1,64]{1,0:T(1,128)}, f32[1,1]{1,0:T(1,128)}) custom-call(f32[64,128]{1,0:T(8,128)S(1)} %bitcast.7, s32[1,64]{1,0:T(1,128)S(1)} %get-tuple-element.9.id_ref), custom_call_target="tpu_custom_call" | custom-call | tf_op jit(solution)/shard_map/pick_proof/pallas_call | solution.py:340
Async XLA Ops:
  1.7 13.5 %collective-permute-start.3 = (f32[392,128]{1,0:T(8,128)S(1)}, f32[392,128]{1,0:T(8,128)S(1)}, u32[]{:S(2)}, u32[]{:S(2)}) collective-permute-start(f32[392,128]{1,0:T(8,128)S(1)} %get-tuple-element.8.refs_0_), channel_id=1, source_target_pairs={{0,24},{1,25},{2,26},{3,27},{4,28},{5,29},{6,30},{7,31},{8,16},{9,... | collective-permute-start | bytes 602120 | tf_op jit(solution)/shard_map/ppermute | solution.py:302
  6.8 8.7 %collective-permute-start.2 = (f32[392,128]{1,0:T(8,128)S(1)}, f32[392,128]{1,0:T(8,128)S(1)}, u32[]{:S(2)}, u32[]{:S(2)}) collective-permute-start(f32[392,128]{1,0:T(8,128)S(1)} %get-tuple-element.8.refs_0_), channel_id=1, source_target_pairs={{0,6},{1,7},{2,4},{3,5},{4,2},{5,3},{6,0},{7,1},{8,14},{9,15},{10,... | collective-permute-start | bytes 602120 | tf_op jit(solution)/shard_map/ppermute | solution.py:302
  9.3 9.3 %collective-permute-start.6 = (f32[392,128]{1,0:T(8,128)S(1)}, f32[392,128]{1,0:T(8,128)S(1)}, u32[]{:S(2)}, u32[]{:S(2)}) collective-permute-start(f32[392,128]{1,0:T(8,128)S(1)} %get-tuple-element.8.refs_0_), channel_id=1, source_target_pairs={{0,9},{1,8},{2,11},{3,10},{4,13},{5,12},{6,15},{7,14},{8,0},{9,1},... | collective-permute-start | bytes 602120 | tf_op jit(solution)/shard_map/ppermute | solution.py:302
  9.3 9.3 %collective-permute-start.1 = (f32[392,128]{1,0:T(8,128)S(1)}, f32[392,128]{1,0:T(8,128)S(1)}, u32[]{:S(2)}, u32[]{:S(2)}) collective-permute-start(f32[392,128]{1,0:T(8,128)S(1)} %get-tuple-element.8.refs_0_), channel_id=1, source_target_pairs={{0,4},{1,5},{2,6},{3,7},{4,0},{5,1},{6,2},{7,3},{8,12},{9,13},{10,... | collective-permute-start | bytes 602120 | tf_op jit(solution)/shard_map/ppermute | solution.py:302
  9.8 8.8 %collective-permute-start = (f32[392,128]{1,0:T(8,128)S(1)}, f32[392,128]{1,0:T(8,128)S(1)}, u32[]{:S(2)}, u32[]{:S(2)}) collective-permute-start(f32[392,128]{1,0:T(8,128)S(1)} %get-tuple-element.8.refs_0_), channel_id=1, source_target_pairs={{0,2},{1,3},{2,0},{3,1},{4,6},{5,7},{6,4},{7,5},{8,10},{9,11},{10,... | collective-permute-start | bytes 602120 | tf_op jit(solution)/shard_map/ppermute | solution.py:302
  15.6 3.0 %collective-permute-start.5 = (f32[392,128]{1,0:T(8,128)S(1)}, f32[392,128]{1,0:T(8,128)S(1)}, u32[]{:S(2)}, u32[]{:S(2)}) collective-permute-start(f32[392,128]{1,0:T(8,128)S(1)} %collective-permute-done.3.refs_5_), channel_id=1, source_target_pairs={{0,1},{1,0},{2,3},{3,2},{4,5},{5,4},{6,7},{7,6},{8,9},{9,8},{10,11... | collective-permute-start | bytes 602120 | tf_op jit(solution)/shard_map/ppermute | solution.py:302
  15.6 3.0 %collective-permute-start.4 = (f32[392,128]{1,0:T(8,128)S(1)}, f32[392,128]{1,0:T(8,128)S(1)}, u32[]{:S(2)}, u32[]{:S(2)}) collective-permute-start(f32[392,128]{1,0:T(8,128)S(1)} %get-tuple-element.8.refs_0_), channel_id=1, source_target_pairs={{0,1},{1,0},{2,3},{3,2},{4,5},{5,4},{6,7},{7,6},{8,9},{9,8},{10,11... | collective-permute-start | bytes 602120 | tf_op jit(solution)/shard_map/ppermute | solution.py:302

commit v6 on v5

--- a/solution.py
+++ b/solution.py
@@ -208,9 +208,9 @@
     out_ref[...] = jnp.where(lane == places + 4, total, result)
 
 
-def last_kernel(layout, samples, per_peer, factor, half_count, got_ref, id_ref, proof_ref, mmd_ref):
-    got = got_ref[...]
+def pick_kernel(layout, per_peer, factor, id_ref, lane_ref, row_ref):
     ids = id_ref[...]
+    samples = ids.shape[1]
     places = layout.places
     plane, place, core = layout.parts(int_div(ids, samples))
     slot = int_mod(ids, per_peer)
@@ -218,15 +218,10 @@
         [place, places + core, jnp.full(core.shape, places + 2, jnp.int32)], axis=1
     )
     lane_of = lax.broadcasted_iota(jnp.int32, (LANES, 3 * samples), 0)
-    picks = jnp.where(lane_of == targets, 1.0, 0.0).astype(jnp.bfloat16)
-    high, mid, low = split3(got)
-    picked = bf16_dot(high, picks, NN_DIMS) + (
-        bf16_dot(mid, picks, NN_DIMS) + bf16_dot(low, picks, NN_DIMS)
-    )
+    lane_ref[...] = jnp.where(lane_of == targets, 1.0, 0.0).astype(jnp.bfloat16)
     row = lax.broadcasted_iota(jnp.int32, (samples, samples), 0)
     src_plane, src_place, src_core = layout.parts(int_div(row, per_peer))
     right_slot = int_mod(row, per_peer) == slot
-    keep_row = right_slot & (src_plane == plane) & (src_core == core)
     right_place = right_slot & (src_place == place)
 
     def sent_to(table):
@@ -235,19 +230,31 @@
             goal = jnp.where(plane == source, target, goal)
         return goal
 
+    keep_row = right_slot & (src_plane == plane) & (src_core == core)
     keep_a = right_place & (src_plane == sent_to(ROUND_A))
     crossing = (plane == CROSSING[0]) | (plane == CROSSING[1])
     keep_b = right_place & (src_plane == sent_to(ROUND_B))
     keep_b = keep_b & (src_core == jnp.where(crossing, 1 - core, core))
-    sums = jnp.where(keep_row, picked[:, :samples], 0.0)
-    sums = sums + jnp.where(keep_a, picked[:, samples : 2 * samples], 0.0)
-    sums = sums + jnp.where(keep_b, picked[:, 2 * samples :], 0.0)
-    proof_ref[...] = jnp.sum(sums, axis=0, keepdims=True) * factor
+    row_ref[...] = jnp.concatenate(
+        [jnp.where(keep, factor, 0.0) for keep in (keep_row, keep_a, keep_b)], axis=1
+    )
+
+
+def last_kernel(layout, per_peer, scale, got_ref, lane_ref, row_ref, proof_ref, mmd_ref):
+    got = got_ref[...]
+    samples = got.shape[0]
+    parts = jnp.concatenate(split3(got), axis=0)
+    picked = bf16_dot(parts, lane_ref[...], NN_DIMS)
+    picked = picked[:samples] + (picked[samples : 2 * samples] + picked[2 * samples :])
+    sums = jnp.sum(picked * row_ref[...], axis=0, keepdims=True)
+    proof_ref[...] = (
+        sums[:, :samples] + sums[:, samples : 2 * samples] + sums[:, 2 * samples :]
+    )
     row = lax.broadcasted_iota(jnp.int32, (samples, LANES), 0)
     lane = lax.broadcasted_iota(jnp.int32, (samples, LANES), 1)
-    is_total = (lane == places + 4) & (int_mod(row, per_peer) == 0)
+    is_total = (lane == layout.places + 4) & (int_mod(row, per_peer) == 0)
     total = jnp.sum(jnp.where(is_total, got, 0.0), axis=(0, 1), keepdims=True)
-    mmd_ref[...] = total * factor * (1.0 / half_count)
+    mmd_ref[...] = total * scale
 
 
 def in_vmem(array):
@@ -320,7 +327,21 @@
     late, *_ = lax.optimization_barrier((packed, in_plane[-1], far_a))
     near = send(late, to_core)
 
+    ids, far_b = lax.optimization_barrier((ids, far_b))
+    lanes, rows = pl.pallas_call(
+        functools.partial(pick_kernel, layout, per_peer, factor),
+        out_shape=(
+            pltpu.VMEM((LANES, 3 * samples), jnp.bfloat16),
+            pltpu.VMEM((samples, 3 * samples), jnp.float32),
+        ),
+        in_specs=vmem_specs(1),
+        out_specs=tuple(vmem_specs(2)),
+        compiler_params=pltpu.CompilerParams(vmem_limit_bytes=16 * MIB),
+        name="pick_masks",
+    )(in_vmem(ids))
+    far_b, lanes, rows = lax.optimization_barrier((far_b, lanes, rows))
     blocks = [packed, *in_plane, near, far_a, far_a_other, far_b]
+
     partial = pl.pallas_call(
         functools.partial(main_kernel, samples, chunks, layout),
         out_shape=pltpu.VMEM((samples, LANES), jnp.float32),
@@ -338,16 +359,16 @@
     got = lax.all_to_all(partial, ("row", "col"), split_axis=0, concat_axis=0, tiled=True)
 
     proof, mmd = pl.pallas_call(
-        functools.partial(last_kernel, layout, samples, per_peer, factor, half_count),
+        functools.partial(last_kernel, layout, per_peer, factor / half_count),
         out_shape=(
             jax.ShapeDtypeStruct((1, samples), jnp.float32),
             jax.ShapeDtypeStruct((1, 1), jnp.float32),
         ),
-        in_specs=vmem_specs(2),
+        in_specs=vmem_specs(3),
         out_specs=tuple(vmem_specs(2)),
         compiler_params=pltpu.CompilerParams(vmem_limit_bytes=16 * MIB),
         name="pick_proof",
-    )(in_vmem(got), in_vmem(ids))
+    )(in_vmem(got), in_vmem(lanes), in_vmem(rows))
     return proof.reshape(samples), mmd.reshape(())
 
 

time: 30.2 us -> 30.1 us (level)
    pallas_call x1 -> x2, Pallas kernels: 0.84 us -> 0.86 us  [the longest x1 0.76 us: local(): pl.pallas_call(functools.partial(last_kernel, layout, per_peer, factor /...]
where the time goes in v6:
time: 30.1 us; the launch traced here: 29.9 us
  blocking collectives  9.43 us (31%)
  starting transfers between devices  9.1 us (30%)
  waiting for transfers between devices  7.76 us (26%)
  Pallas kernels  2.93 us (10%)
  between operations  0.68 us (2%)
    all_to_all x1, blocking collectives, local(): lax.all_to_all(partial, ('row', 'col'), split_axis=0, concat_axis=0, tile...  9.43 us
    ppermute x7, starting transfers between devices, send(): return lax.ppermute(block, ('row', 'col'), layout.pairs(target))  9.1 us
    ppermute x7, waiting for transfers between devices, send(): return lax.ppermute(block, ('row', 'col'), layout.pairs(target))  7.76 us
    pallas_call x1, Pallas kernels, local(): pl.pallas_call(pack_kernel, out_shape=(pltpu.VMEM((pack_rows, LANES), jnp...  1.07 us
    pallas_call x1, Pallas kernels, local(): pl.pallas_call(functools.partial(main_kernel, samples, chunks, layout), o...  1 us
    pallas_call x1, Pallas kernels, local(): pl.pallas_call(functools.partial(last_kernel, layout, per_peer, factor /...  0.76 us
  transfers between devices with their start and end apart: 7, of which 3 were waited for; matrix products, arithmetic and copies ran while one was open for 0% of the time, Pallas kernels for 0%

profile of v6, /device:TPU:0, one launch (start us, length us, event | category | flops | bytes accessed | tf_op | source)
XLA Modules:
  0.0 29.9 jit_solution(6930345101706216035)
XLA Ops:
  0.6 1.1 %pack_block.1 = (f32[392,128]{1,0:T(8,128)S(1)}, s32[1,64]{1,0:T(1,128)S(1)}) custom-call(f32[64,768]{1,0:T(8,128)} %emb_ref.1, s32[1,64]{1,0:T(1,128)} %bitcast.8, s32[1,64]{1,0:T(1,128)} %bitcast.9), custom_call_target="tpu_custom_call" | custom-call | tf_op jit(solution)/shard_map/pack_block/pallas_call | solution.py:288
  1.7 5.1 %collective-permute-start.3 = (f32[392,128]{1,0:T(8,128)S(1)}, f32[392,128]{1,0:T(8,128)S(1)}, u32[]{:S(2)}, u32[]{:S(2)}) collective-permute-start(f32[392,128]{1,0:T(8,128)S(1)} %get-tuple-element.15.refs_0_), channel_id=1, source_target_pairs={{0,24},{1,25},{2,26},{3,27},{4,28},{5,29},{6,30},{7,31},{8,16},{9,... | collective-permute-start | bytes 602120 | tf_op jit(solution)/shard_map/ppermute | solution.py:309
  6.8 2.4 %collective-permute-start.2 = (f32[392,128]{1,0:T(8,128)S(1)}, f32[392,128]{1,0:T(8,128)S(1)}, u32[]{:S(2)}, u32[]{:S(2)}) collective-permute-start(f32[392,128]{1,0:T(8,128)S(1)} %get-tuple-element.15.refs_0_), channel_id=1, source_target_pairs={{0,6},{1,7},{2,4},{3,5},{4,2},{5,3},{6,0},{7,1},{8,14},{9,15},{10,... | collective-permute-start | bytes 602120 | tf_op jit(solution)/shard_map/ppermute | solution.py:309
  9.3 0.0 collective-permute-start.6
  9.3 0.5 %collective-permute-start.1 = (f32[392,128]{1,0:T(8,128)S(1)}, f32[392,128]{1,0:T(8,128)S(1)}, u32[]{:S(2)}, u32[]{:S(2)}) collective-permute-start(f32[392,128]{1,0:T(8,128)S(1)} %get-tuple-element.15.refs_0_), channel_id=1, source_target_pairs={{0,4},{1,5},{2,6},{3,7},{4,0},{5,1},{6,2},{7,3},{8,12},{9,13},{10,... | collective-permute-start | bytes 602120 | tf_op jit(solution)/shard_map/ppermute | solution.py:309
  9.8 0.5 %collective-permute-start = (f32[392,128]{1,0:T(8,128)S(1)}, f32[392,128]{1,0:T(8,128)S(1)}, u32[]{:S(2)}, u32[]{:S(2)}) collective-permute-start(f32[392,128]{1,0:T(8,128)S(1)} %get-tuple-element.15.refs_0_), channel_id=1, source_target_pairs={{0,2},{1,3},{2,0},{3,1},{4,6},{5,7},{6,4},{7,5},{8,10},{9,11},{10,... | collective-permute-start | bytes 602120 | tf_op jit(solution)/shard_map/ppermute | solution.py:309
  10.3 4.9 %collective-permute-done.3.refs_5_ = f32[392,128]{1,0:T(8,128)S(1)} collective-permute-done((f32[392,128]{1,0:T(8,128)S(1)}, f32[392,128]{1,0:T(8,128)S(1)}, u32[]{:S(2)}, u32[]{:S(2)}) %collective-permute-start.3) | collective-permute-done | bytes 200736 | tf_op jit(solution)/shard_map/ppermute | solution.py:309
  15.2 0.4 %collective-permute-done.2.refs_3_ = f32[392,128]{1,0:T(8,128)S(1)} collective-permute-done((f32[392,128]{1,0:T(8,128)S(1)}, f32[392,128]{1,0:T(8,128)S(1)}, u32[]{:S(2)}, u32[]{:S(2)}) %collective-permute-start.2) | collective-permute-done | bytes 200736 | tf_op jit(solution)/shard_map/ppermute | solution.py:309
  15.6 0.0 collective-permute-start.5
  15.6 0.5 %collective-permute-start.4 = (f32[392,128]{1,0:T(8,128)S(1)}, f32[392,128]{1,0:T(8,128)S(1)}, u32[]{:S(2)}, u32[]{:S(2)}) collective-permute-start(f32[392,128]{1,0:T(8,128)S(1)} %get-tuple-element.15.refs_0_), channel_id=1, source_target_pairs={{0,1},{1,0},{2,3},{3,2},{4,5},{5,4},{6,7},{7,6},{8,9},{9,8},{10,11... | collective-permute-start | bytes 602120 | tf_op jit(solution)/shard_map/ppermute | solution.py:309
  16.1 2.5 %collective-permute-done.6.refs_7_ = f32[392,128]{1,0:T(8,128)S(1)} collective-permute-done((f32[392,128]{1,0:T(8,128)S(1)}, f32[392,128]{1,0:T(8,128)S(1)}, u32[]{:S(2)}, u32[]{:S(2)}) %collective-permute-start.6) | collective-permute-done | bytes 200736 | tf_op jit(solution)/shard_map/ppermute | solution.py:309
  18.6 0.1 pick_masks.1
  18.7 0.0 collective-permute-done.1.refs_2_
  18.7 0.0 collective-permute-done.refs_1_
  18.7 0.0 collective-permute-done.5.refs_6_
  18.7 0.0 collective-permute-done.4.refs_4_
  18.7 1.0 %kernel_sums.1 = f32[64,128]{1,0:T(8,128)S(1)} custom-call(f32[392,128]{1,0:T(8,128)S(1)} %get-tuple-element.15.refs_0_, f32[392,128]{1,0:T(8,128)S(1)} %collective-permute-done.refs_1_, f32[392,128]{1,0:T(8,128)S(1)} %collective-permute-done.1.refs_2_, f32[392,128]{1,0:T(8,128)S(1)} %collective-permute-done.2.refs_3_, ...), custom_call_target="tpu_custom_call" | custom-call | tf_op jit(solution)/shard_map/kernel_sums/pallas_call | solution.py:345
  19.7 9.4 %all_to_all.11 = f32[32,2,128]{2,1,0:T(2,128)S(1)} all-to-all(f32[32,2,128]{2,1,0:T(2,128)S(1)} %bitcast.6), channel_id=1, replica_groups=mesh['row'=4,'col'=8] {'row','col'}, dimensions={0} | all-to-all | bytes 65536 | tf_op jit(solution)/shard_map/all_to_all | solution.py:359
  29.2 0.8 %pick_proof.1 = (f32[1,64]{1,0:T(1,128)}, f32[1,1]{1,0:T(1,128)}) custom-call(f32[64,128]{1,0:T(8,128)S(1)} %bitcast.7, bf16[128,192]{1,0:T(8,128)(2,1)S(1)} %get-tuple-element.22.lane_ref, f32[64,192]{1,0:T(8,128)S(1)} %get-tuple-element.23.row_ref), custom_call_target="tpu_custom_call" | custom-call | tf_op jit(solution)/shard_map/pick_proof/pallas_call | solution.py:361
Async XLA Ops:
  1.7 13.5 %collective-permute-start.3 = (f32[392,128]{1,0:T(8,128)S(1)}, f32[392,128]{1,0:T(8,128)S(1)}, u32[]{:S(2)}, u32[]{:S(2)}) collective-permute-start(f32[392,128]{1,0:T(8,128)S(1)} %get-tuple-element.15.refs_0_), channel_id=1, source_target_pairs={{0,24},{1,25},{2,26},{3,27},{4,28},{5,29},{6,30},{7,31},{8,16},{9,... | collective-permute-start | bytes 602120 | tf_op jit(solution)/shard_map/ppermute | solution.py:309
  6.8 8.7 %collective-permute-start.2 = (f32[392,128]{1,0:T(8,128)S(1)}, f32[392,128]{1,0:T(8,128)S(1)}, u32[]{:S(2)}, u32[]{:S(2)}) collective-permute-start(f32[392,128]{1,0:T(8,128)S(1)} %get-tuple-element.15.refs_0_), channel_id=1, source_target_pairs={{0,6},{1,7},{2,4},{3,5},{4,2},{5,3},{6,0},{7,1},{8,14},{9,15},{10,... | collective-permute-start | bytes 602120 | tf_op jit(solution)/shard_map/ppermute | solution.py:309
  9.3 9.3 %collective-permute-start.6 = (f32[392,128]{1,0:T(8,128)S(1)}, f32[392,128]{1,0:T(8,128)S(1)}, u32[]{:S(2)}, u32[]{:S(2)}) collective-permute-start(f32[392,128]{1,0:T(8,128)S(1)} %get-tuple-element.15.refs_0_), channel_id=1, source_target_pairs={{0,9},{1,8},{2,11},{3,10},{4,13},{5,12},{6,15},{7,14},{8,0},{9,1},... | collective-permute-start | bytes 602120 | tf_op jit(solution)/shard_map/ppermute | solution.py:309
  9.3 9.4 %collective-permute-start.1 = (f32[392,128]{1,0:T(8,128)S(1)}, f32[392,128]{1,0:T(8,128)S(1)}, u32[]{:S(2)}, u32[]{:S(2)}) collective-permute-start(f32[392,128]{1,0:T(8,128)S(1)} %get-tuple-element.15.refs_0_), channel_id=1, source_target_pairs={{0,4},{1,5},{2,6},{3,7},{4,0},{5,1},{6,2},{7,3},{8,12},{9,13},{10,... | collective-permute-start | bytes 602120 | tf_op jit(solution)/shard_map/ppermute | solution.py:309
  9.8 8.9 %collective-permute-start = (f32[392,128]{1,0:T(8,128)S(1)}, f32[392,128]{1,0:T(8,128)S(1)}, u32[]{:S(2)}, u32[]{:S(2)}) collective-permute-start(f32[392,128]{1,0:T(8,128)S(1)} %get-tuple-element.15.refs_0_), channel_id=1, source_target_pairs={{0,2},{1,3},{2,0},{3,1},{4,6},{5,7},{6,4},{7,5},{8,10},{9,11},{10,... | collective-permute-start | bytes 602120 | tf_op jit(solution)/shard_map/ppermute | solution.py:309
  15.6 3.1 %collective-permute-start.5 = (f32[392,128]{1,0:T(8,128)S(1)}, f32[392,128]{1,0:T(8,128)S(1)}, u32[]{:S(2)}, u32[]{:S(2)}) collective-permute-start(f32[392,128]{1,0:T(8,128)S(1)} %collective-permute-done.3.refs_5_), channel_id=1, source_target_pairs={{0,1},{1,0},{2,3},{3,2},{4,5},{5,4},{6,7},{7,6},{8,9},{9,8},{10,11... | collective-permute-start | bytes 602120 | tf_op jit(solution)/shard_map/ppermute | solution.py:309
  15.6 3.1 %collective-permute-start.4 = (f32[392,128]{1,0:T(8,128)S(1)}, f32[392,128]{1,0:T(8,128)S(1)}, u32[]{:S(2)}, u32[]{:S(2)}) collective-permute-start(f32[392,128]{1,0:T(8,128)S(1)} %get-tuple-element.15.refs_0_), channel_id=1, source_target_pairs={{0,1},{1,0},{2,3},{3,2},{4,5},{5,4},{6,7},{7,6},{8,9},{9,8},{10,11... | collective-permute-start | bytes 602120 | tf_op jit(solution)/shard_map/ppermute | solution.py:309

commit v7 on v6

--- a/solution.py
+++ b/solution.py
@@ -121,11 +121,12 @@
     copies[chunks + 1].wait()
 
 
-def stage(ref, scratch, start, middle, samples, chunks):
+def stage(ref, scratch, start, order, samples, chunks):
     for chunk in range(chunks):
-        value = ref[pl.ds(chunk * samples, samples), :]
-        for offset, piece in zip((0, middle), split2(value)):
-            scratch[pl.ds(offset + start, samples), pl.ds(chunk * LANES, LANES)] = piece
+        pieces = split2(ref[pl.ds(chunk * samples, samples), :])
+        for place, part in enumerate(order):
+            lanes = pl.ds((place * chunks + chunk) * LANES, LANES)
+            scratch[pl.ds(start, samples), lanes] = pieces[part]
 
 
 def tail_rows(refs, samples, chunks):
@@ -153,14 +154,13 @@
     out_ref, key_parts, query_parts, tail_ref = refs[places + 4 :]
     _, me_place, me_core = layout.here()
     rows = places * samples
-    key_rows = len(keys) * samples
     group = min(GROUP_ROWS, rows)
     blocks = group // samples
     near = CORES * samples
     for place, ref in enumerate(queries):
-        stage(ref, query_parts, place * samples, rows, samples, chunks)
+        stage(ref, query_parts, place * samples, (0, 0, 1, 1), samples, chunks)
     for place, ref in enumerate(keys):
-        stage(ref, key_parts, place * samples, key_rows, samples, chunks)
+        stage(ref, key_parts, place * samples, (0, 1, 0, 1), samples, chunks)
     key_tail = as_columns(tail_rows(keys, samples, chunks))
     key_sign, key_norm = key_tail[:, 0:1], key_tail[:, 1:2]
     tail_ref[...] = tail_rows(queries, samples, chunks)
@@ -169,10 +169,7 @@
     def one_group(index, carry):
         result, total, column = carry
         start = pl.multiple_of(index * group, group)
-        both = key_parts[...]
-        by_high = bf16_dot(both, query_parts[pl.ds(start, group), :], NT_DIMS)
-        by_mid = bf16_dot(both, query_parts[pl.ds(rows + start, group), :], NT_DIMS)
-        inner = by_high[:key_rows] + (by_high[key_rows:] + by_mid[:key_rows] + by_mid[key_rows:])
+        inner = bf16_dot(key_parts[...], query_parts[pl.ds(start, group), :], NT_DIMS)
         sign = tail_ref[0:1, pl.ds(start, group)]
         norm = tail_ref[1:2, pl.ds(start, group)]
         sq_dist = norm + key_norm - 2.0 * inner
@@ -282,7 +279,7 @@
     key_rows = (CORES + FAR_BLOCKS) * samples
     query_rows = places * samples
     block_bytes = pack_rows * LANES * 4
-    work_bytes = (key_rows + query_rows) * width * 6 + 8 * GROUP_ROWS * key_rows * 4
+    work_bytes = (key_rows + query_rows) * width * 8 + 4 * GROUP_ROWS * key_rows * 4
     params = pltpu.CompilerParams(vmem_limit_bytes=work_bytes + 4 * MIB)
 
     packed, ids = pl.pallas_call(
@@ -348,8 +345,8 @@
         in_specs=vmem_specs(len(blocks)),
         out_specs=pl.BlockSpec(memory_space=pltpu.VMEM),
         scratch_shapes=[
-            pltpu.VMEM((2 * key_rows, width), jnp.bfloat16),
-            pltpu.VMEM((2 * query_rows, width), jnp.bfloat16),
+            pltpu.VMEM((key_rows, 4 * width), jnp.bfloat16),
+            pltpu.VMEM((query_rows, 4 * width), jnp.bfloat16),
             pltpu.VMEM((SUBLANES, query_rows), jnp.float32),
         ],
         compiler_params=params,

time: 30.1 us -> 30.2 us (level)
  no operation moved by 1% of the time
where the time goes in v7:
time: 30.2 us; the launch traced here: 30 us
  blocking collectives  9.43 us (31%)
  starting transfers between devices  9.1 us (30%)
  waiting for transfers between devices  7.76 us (26%)
  Pallas kernels  3.02 us (10%)
  between operations  0.68 us (2%)
    all_to_all x1, blocking collectives, local(): lax.all_to_all(partial, ('row', 'col'), split_axis=0, concat_axis=0, tile...  9.43 us
    ppermute x7, starting transfers between devices, send(): return lax.ppermute(block, ('row', 'col'), layout.pairs(target))  9.1 us
    ppermute x7, waiting for transfers between devices, send(): return lax.ppermute(block, ('row', 'col'), layout.pairs(target))  7.76 us
    pallas_call x1, Pallas kernels, local(): pl.pallas_call(functools.partial(main_kernel, samples, chunks, layout), o...  1.09 us
    pallas_call x1, Pallas kernels, local(): pl.pallas_call(pack_kernel, out_shape=(pltpu.VMEM((pack_rows, LANES), jnp...  1.07 us
    pallas_call x1, Pallas kernels, local(): pl.pallas_call(functools.partial(last_kernel, layout, per_peer, factor /...  0.76 us
  transfers between devices with their start and end apart: 7, of which 3 were waited for; matrix products, arithmetic and copies ran while one was open for 0% of the time, Pallas kernels for 0%

profile of v7, /device:TPU:0, one launch (start us, length us, event | category | flops | bytes accessed | tf_op | source)
XLA Modules:
  0.0 30.0 jit_solution(14869058939836628866)
XLA Ops:
  0.6 1.1 %pack_block.1 = (f32[392,128]{1,0:T(8,128)S(1)}, s32[1,64]{1,0:T(1,128)S(1)}) custom-call(f32[64,768]{1,0:T(8,128)} %emb_ref.1, s32[1,64]{1,0:T(1,128)} %bitcast.8, s32[1,64]{1,0:T(1,128)} %bitcast.9), custom_call_target="tpu_custom_call" | custom-call | tf_op jit(solution)/shard_map/pack_block/pallas_call | solution.py:285
  1.7 5.1 %collective-permute-start.3 = (f32[392,128]{1,0:T(8,128)S(1)}, f32[392,128]{1,0:T(8,128)S(1)}, u32[]{:S(2)}, u32[]{:S(2)}) collective-permute-start(f32[392,128]{1,0:T(8,128)S(1)} %get-tuple-element.15.refs_0_), channel_id=1, source_target_pairs={{0,24},{1,25},{2,26},{3,27},{4,28},{5,29},{6,30},{7,31},{8,16},{9,... | collective-permute-start | bytes 602120 | tf_op jit(solution)/shard_map/ppermute | solution.py:306
  6.8 2.4 %collective-permute-start.2 = (f32[392,128]{1,0:T(8,128)S(1)}, f32[392,128]{1,0:T(8,128)S(1)}, u32[]{:S(2)}, u32[]{:S(2)}) collective-permute-start(f32[392,128]{1,0:T(8,128)S(1)} %get-tuple-element.15.refs_0_), channel_id=1, source_target_pairs={{0,6},{1,7},{2,4},{3,5},{4,2},{5,3},{6,0},{7,1},{8,14},{9,15},{10,... | collective-permute-start | bytes 602120 | tf_op jit(solution)/shard_map/ppermute | solution.py:306
  9.3 0.0 collective-permute-start.6
  9.3 0.5 %collective-permute-start.1 = (f32[392,128]{1,0:T(8,128)S(1)}, f32[392,128]{1,0:T(8,128)S(1)}, u32[]{:S(2)}, u32[]{:S(2)}) collective-permute-start(f32[392,128]{1,0:T(8,128)S(1)} %get-tuple-element.15.refs_0_), channel_id=1, source_target_pairs={{0,4},{1,5},{2,6},{3,7},{4,0},{5,1},{6,2},{7,3},{8,12},{9,13},{10,... | collective-permute-start | bytes 602120 | tf_op jit(solution)/shard_map/ppermute | solution.py:306
  9.8 0.5 %collective-permute-start = (f32[392,128]{1,0:T(8,128)S(1)}, f32[392,128]{1,0:T(8,128)S(1)}, u32[]{:S(2)}, u32[]{:S(2)}) collective-permute-start(f32[392,128]{1,0:T(8,128)S(1)} %get-tuple-element.15.refs_0_), channel_id=1, source_target_pairs={{0,2},{1,3},{2,0},{3,1},{4,6},{5,7},{6,4},{7,5},{8,10},{9,11},{10,... | collective-permute-start | bytes 602120 | tf_op jit(solution)/shard_map/ppermute | solution.py:306
  10.3 4.9 %collective-permute-done.3.refs_5_ = f32[392,128]{1,0:T(8,128)S(1)} collective-permute-done((f32[392,128]{1,0:T(8,128)S(1)}, f32[392,128]{1,0:T(8,128)S(1)}, u32[]{:S(2)}, u32[]{:S(2)}) %collective-permute-start.3) | collective-permute-done | bytes 200736 | tf_op jit(solution)/shard_map/ppermute | solution.py:306
  15.2 0.4 %collective-permute-done.2.refs_3_ = f32[392,128]{1,0:T(8,128)S(1)} collective-permute-done((f32[392,128]{1,0:T(8,128)S(1)}, f32[392,128]{1,0:T(8,128)S(1)}, u32[]{:S(2)}, u32[]{:S(2)}) %collective-permute-start.2) | collective-permute-done | bytes 200736 | tf_op jit(solution)/shard_map/ppermute | solution.py:306
  15.6 0.0 collective-permute-start.5
  15.6 0.5 %collective-permute-start.4 = (f32[392,128]{1,0:T(8,128)S(1)}, f32[392,128]{1,0:T(8,128)S(1)}, u32[]{:S(2)}, u32[]{:S(2)}) collective-permute-start(f32[392,128]{1,0:T(8,128)S(1)} %get-tuple-element.15.refs_0_), channel_id=1, source_target_pairs={{0,1},{1,0},{2,3},{3,2},{4,5},{5,4},{6,7},{7,6},{8,9},{9,8},{10,11... | collective-permute-start | bytes 602120 | tf_op jit(solution)/shard_map/ppermute | solution.py:306
  16.1 2.5 %collective-permute-done.6.refs_7_ = f32[392,128]{1,0:T(8,128)S(1)} collective-permute-done((f32[392,128]{1,0:T(8,128)S(1)}, f32[392,128]{1,0:T(8,128)S(1)}, u32[]{:S(2)}, u32[]{:S(2)}) %collective-permute-start.6) | collective-permute-done | bytes 200736 | tf_op jit(solution)/shard_map/ppermute | solution.py:306
  18.6 0.1 pick_masks.1
  18.7 0.0 collective-permute-done.1.refs_2_
  18.7 0.0 collective-permute-done.refs_1_
  18.7 0.0 collective-permute-done.5.refs_6_
  18.7 0.0 collective-permute-done.4.refs_4_
  18.7 1.1 %kernel_sums.1 = f32[64,128]{1,0:T(8,128)S(1)} custom-call(f32[392,128]{1,0:T(8,128)S(1)} %get-tuple-element.15.refs_0_, f32[392,128]{1,0:T(8,128)S(1)} %collective-permute-done.refs_1_, f32[392,128]{1,0:T(8,128)S(1)} %collective-permute-done.1.refs_2_, f32[392,128]{1,0:T(8,128)S(1)} %collective-permute-done.2.refs_3_, ...), custom_call_target="tpu_custom_call" | custom-call | tf_op jit(solution)/shard_map/kernel_sums/pallas_call | solution.py:342
  19.8 9.4 %all_to_all.11 = f32[32,2,128]{2,1,0:T(2,128)S(1)} all-to-all(f32[32,2,128]{2,1,0:T(2,128)S(1)} %bitcast.6), channel_id=1, replica_groups=mesh['row'=4,'col'=8] {'row','col'}, dimensions={0} | all-to-all | bytes 65536 | tf_op jit(solution)/shard_map/all_to_all | solution.py:356
  29.2 0.8 %pick_proof.1 = (f32[1,64]{1,0:T(1,128)}, f32[1,1]{1,0:T(1,128)}) custom-call(f32[64,128]{1,0:T(8,128)S(1)} %bitcast.7, bf16[128,192]{1,0:T(8,128)(2,1)S(1)} %get-tuple-element.22.lane_ref, f32[64,192]{1,0:T(8,128)S(1)} %get-tuple-element.23.row_ref), custom_call_target="tpu_custom_call" | custom-call | tf_op jit(solution)/shard_map/pick_proof/pallas_call | solution.py:358
Async XLA Ops:
  1.7 13.5 %collective-permute-start.3 = (f32[392,128]{1,0:T(8,128)S(1)}, f32[392,128]{1,0:T(8,128)S(1)}, u32[]{:S(2)}, u32[]{:S(2)}) collective-permute-start(f32[392,128]{1,0:T(8,128)S(1)} %get-tuple-element.15.refs_0_), channel_id=1, source_target_pairs={{0,24},{1,25},{2,26},{3,27},{4,28},{5,29},{6,30},{7,31},{8,16},{9,... | collective-permute-start | bytes 602120 | tf_op jit(solution)/shard_map/ppermute | solution.py:306
  6.8 8.7 %collective-permute-start.2 = (f32[392,128]{1,0:T(8,128)S(1)}, f32[392,128]{1,0:T(8,128)S(1)}, u32[]{:S(2)}, u32[]{:S(2)}) collective-permute-start(f32[392,128]{1,0:T(8,128)S(1)} %get-tuple-element.15.refs_0_), channel_id=1, source_target_pairs={{0,6},{1,7},{2,4},{3,5},{4,2},{5,3},{6,0},{7,1},{8,14},{9,15},{10,... | collective-permute-start | bytes 602120 | tf_op jit(solution)/shard_map/ppermute | solution.py:306
  9.3 9.3 %collective-permute-start.6 = (f32[392,128]{1,0:T(8,128)S(1)}, f32[392,128]{1,0:T(8,128)S(1)}, u32[]{:S(2)}, u32[]{:S(2)}) collective-permute-start(f32[392,128]{1,0:T(8,128)S(1)} %get-tuple-element.15.refs_0_), channel_id=1, source_target_pairs={{0,9},{1,8},{2,11},{3,10},{4,13},{5,12},{6,15},{7,14},{8,0},{9,1},... | collective-permute-start | bytes 602120 | tf_op jit(solution)/shard_map/ppermute | solution.py:306
  9.3 9.4 %collective-permute-start.1 = (f32[392,128]{1,0:T(8,128)S(1)}, f32[392,128]{1,0:T(8,128)S(1)}, u32[]{:S(2)}, u32[]{:S(2)}) collective-permute-start(f32[392,128]{1,0:T(8,128)S(1)} %get-tuple-element.15.refs_0_), channel_id=1, source_target_pairs={{0,4},{1,5},{2,6},{3,7},{4,0},{5,1},{6,2},{7,3},{8,12},{9,13},{10,... | collective-permute-start | bytes 602120 | tf_op jit(solution)/shard_map/ppermute | solution.py:306
  9.8 8.9 %collective-permute-start = (f32[392,128]{1,0:T(8,128)S(1)}, f32[392,128]{1,0:T(8,128)S(1)}, u32[]{:S(2)}, u32[]{:S(2)}) collective-permute-start(f32[392,128]{1,0:T(8,128)S(1)} %get-tuple-element.15.refs_0_), channel_id=1, source_target_pairs={{0,2},{1,3},{2,0},{3,1},{4,6},{5,7},{6,4},{7,5},{8,10},{9,11},{10,... | collective-permute-start | bytes 602120 | tf_op jit(solution)/shard_map/ppermute | solution.py:306
  15.6 3.1 %collective-permute-start.5 = (f32[392,128]{1,0:T(8,128)S(1)}, f32[392,128]{1,0:T(8,128)S(1)}, u32[]{:S(2)}, u32[]{:S(2)}) collective-permute-start(f32[392,128]{1,0:T(8,128)S(1)} %collective-permute-done.3.refs_5_), channel_id=1, source_target_pairs={{0,1},{1,0},{2,3},{3,2},{4,5},{5,4},{6,7},{7,6},{8,9},{9,8},{10,11... | collective-permute-start | bytes 602120 | tf_op jit(solution)/shard_map/ppermute | solution.py:306
  15.6 3.1 %collective-permute-start.4 = (f32[392,128]{1,0:T(8,128)S(1)}, f32[392,128]{1,0:T(8,128)S(1)}, u32[]{:S(2)}, u32[]{:S(2)}) collective-permute-start(f32[392,128]{1,0:T(8,128)S(1)} %get-tuple-element.15.refs_0_), channel_id=1, source_target_pairs={{0,1},{1,0},{2,3},{3,2},{4,5},{5,4},{6,7},{7,6},{8,9},{9,8},{10,11... | collective-permute-start | bytes 602120 | tf_op jit(solution)/shard_map/ppermute | solution.py:306

commit v8 on v6

--- a/solution.py
+++ b/solution.py
@@ -323,8 +323,9 @@
     in_plane = [send(packed, to_place(step)) for step in range(1, places)]
     far_b = send(packed, round_b)
     far_a = send(packed, round_a)
-    far_a_other = send(far_a, to_core)
-    late, *_ = lax.optimization_barrier((packed, in_plane[-1], far_a))
+    late_a, *_ = lax.optimization_barrier((far_a, in_plane[1]))
+    far_a_other = send(late_a, to_core)
+    late, *_ = lax.optimization_barrier((packed, in_plane[1]))
     near = send(late, to_core)
 
     ids, far_b = lax.optimization_barrier((ids, far_b))

time: 30.1 us -> 31.8 us (1.056)
  blocking collectives: 9.43 us -> 10.5 us
  waiting for transfers between devices: 7.76 us -> 8.37 us
    all_to_all x1, blocking collectives: 9.43 us -> 10.5 us  [local(): lax.all_to_all(partial, ('row', 'col'), split_axis=0, concat_axis=0, tile...]
    ppermute x7, waiting for transfers between devices: 7.76 us -> 8.37 us  [send(): return lax.ppermute(block, ('row', 'col'), layout.pairs(target))]
  transfers between devices with their start and end apart: 7 -> 7, of which waited for: 3 -> 4; matrix products, arithmetic and copies ran while one was open for 0% -> 0% of each run, Pallas kernels for 0% -> 0%
where the time goes in v8:
time: 31.8 us; the launch traced here: 31.6 us
  blocking collectives  10.5 us (33%)
  starting transfers between devices  9.1 us (29%)
  waiting for transfers between devices  8.37 us (26%)
  Pallas kernels  2.94 us (9%)
  between operations  0.66 us (2%)
    all_to_all x1, blocking collectives, local(): lax.all_to_all(partial, ('row', 'col'), split_axis=0, concat_axis=0, tile...  10.5 us
    ppermute x7, starting transfers between devices, send(): return lax.ppermute(block, ('row', 'col'), layout.pairs(target))  9.1 us
    ppermute x7, waiting for transfers between devices, send(): return lax.ppermute(block, ('row', 'col'), layout.pairs(target))  8.37 us
    pallas_call x1, Pallas kernels, local(): pl.pallas_call(pack_kernel, out_shape=(pltpu.VMEM((pack_rows, LANES), jnp...  1.07 us
    pallas_call x1, Pallas kernels, local(): pl.pallas_call(functools.partial(main_kernel, samples, chunks, layout), o...  1.01 us
    pallas_call x1, Pallas kernels, local(): pl.pallas_call(functools.partial(last_kernel, layout, per_peer, factor /...  0.76 us
  transfers between devices with their start and end apart: 7, of which 4 were waited for; matrix products, arithmetic and copies ran while one was open for 0% of the time, Pallas kernels for 0%

profile of v8, /device:TPU:0, one launch (start us, length us, event | category | flops | bytes accessed | tf_op | source)
XLA Modules:
  0.0 31.6 jit_solution(10480469523214266191)
XLA Ops:
  0.6 1.1 %pack_block.1 = (f32[392,128]{1,0:T(8,128)S(1)}, s32[1,64]{1,0:T(1,128)S(1)}) custom-call(f32[64,768]{1,0:T(8,128)} %emb_ref.1, s32[1,64]{1,0:T(1,128)} %bitcast.8, s32[1,64]{1,0:T(1,128)} %bitcast.9), custom_call_target="tpu_custom_call" | custom-call | tf_op jit(solution)/shard_map/pack_block/pallas_call | solution.py:288
  1.7 5.1 %collective-permute-start.4 = (f32[392,128]{1,0:T(8,128)S(1)}, f32[392,128]{1,0:T(8,128)S(1)}, u32[]{:S(2)}, u32[]{:S(2)}) collective-permute-start(f32[392,128]{1,0:T(8,128)S(1)} %get-tuple-element.16.refs_0_), channel_id=1, source_target_pairs={{0,24},{1,25},{2,26},{3,27},{4,28},{5,29},{6,30},{7,31},{8,16},{9,... | collective-permute-start | bytes 602120 | tf_op jit(solution)/shard_map/ppermute | solution.py:309
  6.8 1.5 %collective-permute-start.1 = (f32[392,128]{1,0:T(8,128)S(1)}, f32[392,128]{1,0:T(8,128)S(1)}, u32[]{:S(2)}, u32[]{:S(2)}) collective-permute-start(f32[392,128]{1,0:T(8,128)S(1)} %get-tuple-element.16.refs_0_), channel_id=1, source_target_pairs={{0,4},{1,5},{2,6},{3,7},{4,0},{5,1},{6,2},{7,3},{8,12},{9,13},{10,... | collective-permute-start | bytes 602120 | tf_op jit(solution)/shard_map/ppermute | solution.py:309
  8.3 0.0 collective-permute-start.6
  8.3 1.4 %collective-permute-start.2 = (f32[392,128]{1,0:T(8,128)S(1)}, f32[392,128]{1,0:T(8,128)S(1)}, u32[]{:S(2)}, u32[]{:S(2)}) collective-permute-start(f32[392,128]{1,0:T(8,128)S(1)} %get-tuple-element.16.refs_0_), channel_id=1, source_target_pairs={{0,6},{1,7},{2,4},{3,5},{4,2},{5,3},{6,0},{7,1},{8,14},{9,15},{10,... | collective-permute-start | bytes 602120 | tf_op jit(solution)/shard_map/ppermute | solution.py:309
  9.8 0.5 %collective-permute-start = (f32[392,128]{1,0:T(8,128)S(1)}, f32[392,128]{1,0:T(8,128)S(1)}, u32[]{:S(2)}, u32[]{:S(2)}) collective-permute-start(f32[392,128]{1,0:T(8,128)S(1)} %get-tuple-element.16.refs_0_), channel_id=1, source_target_pairs={{0,2},{1,3},{2,0},{3,1},{4,6},{5,7},{6,4},{7,5},{8,10},{9,11},{10,... | collective-permute-start | bytes 602120 | tf_op jit(solution)/shard_map/ppermute | solution.py:309
  10.3 4.9 %collective-permute-done.4.refs_5_ = f32[392,128]{1,0:T(8,128)S(1)} collective-permute-done((f32[392,128]{1,0:T(8,128)S(1)}, f32[392,128]{1,0:T(8,128)S(1)}, u32[]{:S(2)}, u32[]{:S(2)}) %collective-permute-start.4) | collective-permute-done | bytes 200736 | tf_op jit(solution)/shard_map/ppermute | solution.py:309
  15.2 2.4 %collective-permute-done.1.refs_2_ = f32[392,128]{1,0:T(8,128)S(1)} collective-permute-done((f32[392,128]{1,0:T(8,128)S(1)}, f32[392,128]{1,0:T(8,128)S(1)}, u32[]{:S(2)}, u32[]{:S(2)}) %collective-permute-start.1) | collective-permute-done | bytes 200736 | tf_op jit(solution)/shard_map/ppermute | solution.py:309
  17.6 0.0 collective-permute-start.3
  17.6 0.5 %collective-permute-start.5 = (f32[392,128]{1,0:T(8,128)S(1)}, f32[392,128]{1,0:T(8,128)S(1)}, u32[]{:S(2)}, u32[]{:S(2)}) collective-permute-start(f32[392,128]{1,0:T(8,128)S(1)} %collective-permute-done.4.refs_5_), channel_id=1, source_target_pairs={{0,1},{1,0},{2,3},{3,2},{4,5},{5,4},{6,7},{7,6},{8,9},{9,8},{10,11... | collective-permute-start | bytes 602120 | tf_op jit(solution)/shard_map/ppermute | solution.py:309
  18.1 0.0 collective-permute-done.6.refs_7_
  18.1 0.1 pick_masks.1
  18.2 0.0 collective-permute-done.2.refs_3_
  18.2 1.0 %collective-permute-done.refs_1_ = f32[392,128]{1,0:T(8,128)S(1)} collective-permute-done((f32[392,128]{1,0:T(8,128)S(1)}, f32[392,128]{1,0:T(8,128)S(1)}, u32[]{:S(2)}, u32[]{:S(2)}) %collective-permute-start) | collective-permute-done | bytes 200736 | tf_op jit(solution)/shard_map/ppermute | solution.py:309
  19.2 0.0 collective-permute-done.3.refs_4_
  19.2 0.1 collective-permute-done.5.refs_6_
  19.3 1.0 %kernel_sums.1 = f32[64,128]{1,0:T(8,128)S(1)} custom-call(f32[392,128]{1,0:T(8,128)S(1)} %get-tuple-element.16.refs_0_, f32[392,128]{1,0:T(8,128)S(1)} %collective-permute-done.refs_1_, f32[392,128]{1,0:T(8,128)S(1)} %collective-permute-done.1.refs_2_, f32[392,128]{1,0:T(8,128)S(1)} %collective-permute-done.2.refs_3_, ...), custom_call_target="tpu_custom_call" | custom-call | tf_op jit(solution)/shard_map/kernel_sums/pallas_call | solution.py:346
  20.3 10.5 %all_to_all.11 = f32[32,2,128]{2,1,0:T(2,128)S(1)} all-to-all(f32[32,2,128]{2,1,0:T(2,128)S(1)} %bitcast.6), channel_id=1, replica_groups=mesh['row'=4,'col'=8] {'row','col'}, dimensions={0} | all-to-all | bytes 65536 | tf_op jit(solution)/shard_map/all_to_all | solution.py:360
  30.8 0.8 %pick_proof.1 = (f32[1,64]{1,0:T(1,128)}, f32[1,1]{1,0:T(1,128)}) custom-call(f32[64,128]{1,0:T(8,128)S(1)} %bitcast.7, bf16[128,192]{1,0:T(8,128)(2,1)S(1)} %get-tuple-element.24.lane_ref, f32[64,192]{1,0:T(8,128)S(1)} %get-tuple-element.25.row_ref), custom_call_target="tpu_custom_call" | custom-call | tf_op jit(solution)/shard_map/pick_proof/pallas_call | solution.py:362
Async XLA Ops:
  1.7 13.5 %collective-permute-start.4 = (f32[392,128]{1,0:T(8,128)S(1)}, f32[392,128]{1,0:T(8,128)S(1)}, u32[]{:S(2)}, u32[]{:S(2)}) collective-permute-start(f32[392,128]{1,0:T(8,128)S(1)} %get-tuple-element.16.refs_0_), channel_id=1, source_target_pairs={{0,24},{1,25},{2,26},{3,27},{4,28},{5,29},{6,30},{7,31},{8,16},{9,... | collective-permute-start | bytes 602120 | tf_op jit(solution)/shard_map/ppermute | solution.py:309
  6.8 10.8 %collective-permute-start.1 = (f32[392,128]{1,0:T(8,128)S(1)}, f32[392,128]{1,0:T(8,128)S(1)}, u32[]{:S(2)}, u32[]{:S(2)}) collective-permute-start(f32[392,128]{1,0:T(8,128)S(1)} %get-tuple-element.16.refs_0_), channel_id=1, source_target_pairs={{0,4},{1,5},{2,6},{3,7},{4,0},{5,1},{6,2},{7,3},{8,12},{9,13},{10,... | collective-permute-start | bytes 602120 | tf_op jit(solution)/shard_map/ppermute | solution.py:309
  8.3 9.7 %collective-permute-start.6 = (f32[392,128]{1,0:T(8,128)S(1)}, f32[392,128]{1,0:T(8,128)S(1)}, u32[]{:S(2)}, u32[]{:S(2)}) collective-permute-start(f32[392,128]{1,0:T(8,128)S(1)} %get-tuple-element.16.refs_0_), channel_id=1, source_target_pairs={{0,9},{1,8},{2,11},{3,10},{4,13},{5,12},{6,15},{7,14},{8,0},{9,1},... | collective-permute-start | bytes 602120 | tf_op jit(solution)/shard_map/ppermute | solution.py:309
  8.3 9.8 %collective-permute-start.2 = (f32[392,128]{1,0:T(8,128)S(1)}, f32[392,128]{1,0:T(8,128)S(1)}, u32[]{:S(2)}, u32[]{:S(2)}) collective-permute-start(f32[392,128]{1,0:T(8,128)S(1)} %get-tuple-element.16.refs_0_), channel_id=1, source_target_pairs={{0,6},{1,7},{2,4},{3,5},{4,2},{5,3},{6,0},{7,1},{8,14},{9,15},{10,... | collective-permute-start | bytes 602120 | tf_op jit(solution)/shard_map/ppermute | solution.py:309
  9.8 9.4 %collective-permute-start = (f32[392,128]{1,0:T(8,128)S(1)}, f32[392,128]{1,0:T(8,128)S(1)}, u32[]{:S(2)}, u32[]{:S(2)}) collective-permute-start(f32[392,128]{1,0:T(8,128)S(1)} %get-tuple-element.16.refs_0_), channel_id=1, source_target_pairs={{0,2},{1,3},{2,0},{3,1},{4,6},{5,7},{6,4},{7,5},{8,10},{9,11},{10,... | collective-permute-start | bytes 602120 | tf_op jit(solution)/shard_map/ppermute | solution.py:309
  17.6 1.6 %collective-permute-start.3 = (f32[392,128]{1,0:T(8,128)S(1)}, f32[392,128]{1,0:T(8,128)S(1)}, u32[]{:S(2)}, u32[]{:S(2)}) collective-permute-start(f32[392,128]{1,0:T(8,128)S(1)} %get-tuple-element.16.refs_0_), channel_id=1, source_target_pairs={{0,1},{1,0},{2,3},{3,2},{4,5},{5,4},{6,7},{7,6},{8,9},{9,8},{10,11... | collective-permute-start | bytes 602120 | tf_op jit(solution)/shard_map/ppermute | solution.py:309
  17.6 1.7 %collective-permute-start.5 = (f32[392,128]{1,0:T(8,128)S(1)}, f32[392,128]{1,0:T(8,128)S(1)}, u32[]{:S(2)}, u32[]{:S(2)}) collective-permute-start(f32[392,128]{1,0:T(8,128)S(1)} %collective-permute-done.4.refs_5_), channel_id=1, source_target_pairs={{0,1},{1,0},{2,3},{3,2},{4,5},{5,4},{6,7},{7,6},{8,9},{9,8},{10,11... | collective-permute-start | bytes 602120 | tf_op jit(solution)/shard_map/ppermute | solution.py:309

commit v9 on v6

--- a/solution.py
+++ b/solution.py
@@ -14,7 +14,7 @@
 CORES = 2
 ROUND_A = {2: 0, 3: 1, 1: 2, 0: 3}
 ROUND_B = {0: 1, 3: 2, 1: 0, 2: 3}
-CROSSING = (0, 3)
+CROSSING = (1, 3)
 FAR_BLOCKS = 3
 MIB = 1024 * 1024
 NT_DIMS = (((1,), (1,)), ((), ()))

time: 30.1 us -> 30.1 us (level)
  waiting for transfers between devices: 7.76 us -> 8.08 us
  blocking collectives: 9.43 us -> 9.12 us
    all_to_all x1, blocking collectives: 9.43 us -> 9.12 us  [local(): lax.all_to_all(partial, ('row', 'col'), split_axis=0, concat_axis=0, tile...]
    ppermute x7, waiting for transfers between devices: 7.76 us -> 8.08 us  [send(): return lax.ppermute(block, ('row', 'col'), layout.pairs(target))]
where the time goes in v9:
time: 30.1 us; the launch traced here: 29.9 us
  blocking collectives  9.12 us (30%)
  starting transfers between devices  9.1 us (30%)
  waiting for transfers between devices  8.08 us (27%)
  Pallas kernels  2.93 us (10%)
  between operations  0.68 us (2%)
    all_to_all x1, blocking collectives, local(): lax.all_to_all(partial, ('row', 'col'), split_axis=0, concat_axis=0, tile...  9.12 us
    ppermute x7, starting transfers between devices, send(): return lax.ppermute(block, ('row', 'col'), layout.pairs(target))  9.1 us
    ppermute x7, waiting for transfers between devices, send(): return lax.ppermute(block, ('row', 'col'), layout.pairs(target))  8.08 us
    pallas_call x1, Pallas kernels, local(): pl.pallas_call(pack_kernel, out_shape=(pltpu.VMEM((pack_rows, LANES), jnp...  1.07 us
    pallas_call x1, Pallas kernels, local(): pl.pallas_call(functools.partial(main_kernel, samples, chunks, layout), o...  1 us
    pallas_call x1, Pallas kernels, local(): pl.pallas_call(functools.partial(last_kernel, layout, per_peer, factor /...  0.76 us
  transfers between devices with their start and end apart: 7, of which 3 were waited for; matrix products, arithmetic and copies ran while one was open for 0% of the time, Pallas kernels for 0%

profile of v9, /device:TPU:0, one launch (start us, length us, event | category | flops | bytes accessed | tf_op | source)
XLA Modules:
  0.0 29.9 jit_solution(8620483299953773900)
XLA Ops:
  0.6 1.1 %pack_block.1 = (f32[392,128]{1,0:T(8,128)S(1)}, s32[1,64]{1,0:T(1,128)S(1)}) custom-call(f32[64,768]{1,0:T(8,128)} %emb_ref.1, s32[1,64]{1,0:T(1,128)} %bitcast.8, s32[1,64]{1,0:T(1,128)} %bitcast.9), custom_call_target="tpu_custom_call" | custom-call | tf_op jit(solution)/shard_map/pack_block/pallas_call | solution.py:288
  1.7 5.1 %collective-permute-start.3 = (f32[392,128]{1,0:T(8,128)S(1)}, f32[392,128]{1,0:T(8,128)S(1)}, u32[]{:S(2)}, u32[]{:S(2)}) collective-permute-start(f32[392,128]{1,0:T(8,128)S(1)} %get-tuple-element.15.refs_0_), channel_id=1, source_target_pairs={{0,24},{1,25},{2,26},{3,27},{4,28},{5,29},{6,30},{7,31},{8,16},{9,... | collective-permute-start | bytes 602120 | tf_op jit(solution)/shard_map/ppermute | solution.py:309
  6.8 2.4 %collective-permute-start.2 = (f32[392,128]{1,0:T(8,128)S(1)}, f32[392,128]{1,0:T(8,128)S(1)}, u32[]{:S(2)}, u32[]{:S(2)}) collective-permute-start(f32[392,128]{1,0:T(8,128)S(1)} %get-tuple-element.15.refs_0_), channel_id=1, source_target_pairs={{0,6},{1,7},{2,4},{3,5},{4,2},{5,3},{6,0},{7,1},{8,14},{9,15},{10,... | collective-permute-start | bytes 602120 | tf_op jit(solution)/shard_map/ppermute | solution.py:309
  9.3 0.0 collective-permute-start.6
  9.3 0.5 %collective-permute-start.1 = (f32[392,128]{1,0:T(8,128)S(1)}, f32[392,128]{1,0:T(8,128)S(1)}, u32[]{:S(2)}, u32[]{:S(2)}) collective-permute-start(f32[392,128]{1,0:T(8,128)S(1)} %get-tuple-element.15.refs_0_), channel_id=1, source_target_pairs={{0,4},{1,5},{2,6},{3,7},{4,0},{5,1},{6,2},{7,3},{8,12},{9,13},{10,... | collective-permute-start | bytes 602120 | tf_op jit(solution)/shard_map/ppermute | solution.py:309
  9.8 0.5 %collective-permute-start = (f32[392,128]{1,0:T(8,128)S(1)}, f32[392,128]{1,0:T(8,128)S(1)}, u32[]{:S(2)}, u32[]{:S(2)}) collective-permute-start(f32[392,128]{1,0:T(8,128)S(1)} %get-tuple-element.15.refs_0_), channel_id=1, source_target_pairs={{0,2},{1,3},{2,0},{3,1},{4,6},{5,7},{6,4},{7,5},{8,10},{9,11},{10,... | collective-permute-start | bytes 602120 | tf_op jit(solution)/shard_map/ppermute | solution.py:309
  10.3 4.9 %collective-permute-done.3.refs_5_ = f32[392,128]{1,0:T(8,128)S(1)} collective-permute-done((f32[392,128]{1,0:T(8,128)S(1)}, f32[392,128]{1,0:T(8,128)S(1)}, u32[]{:S(2)}, u32[]{:S(2)}) %collective-permute-start.3) | collective-permute-done | bytes 200736 | tf_op jit(solution)/shard_map/ppermute | solution.py:309
  15.2 0.4 %collective-permute-done.2.refs_3_ = f32[392,128]{1,0:T(8,128)S(1)} collective-permute-done((f32[392,128]{1,0:T(8,128)S(1)}, f32[392,128]{1,0:T(8,128)S(1)}, u32[]{:S(2)}, u32[]{:S(2)}) %collective-permute-start.2) | collective-permute-done | bytes 200736 | tf_op jit(solution)/shard_map/ppermute | solution.py:309
  15.6 0.0 collective-permute-start.5
  15.6 0.5 %collective-permute-start.4 = (f32[392,128]{1,0:T(8,128)S(1)}, f32[392,128]{1,0:T(8,128)S(1)}, u32[]{:S(2)}, u32[]{:S(2)}) collective-permute-start(f32[392,128]{1,0:T(8,128)S(1)} %get-tuple-element.15.refs_0_), channel_id=1, source_target_pairs={{0,1},{1,0},{2,3},{3,2},{4,5},{5,4},{6,7},{7,6},{8,9},{9,8},{10,11... | collective-permute-start | bytes 602120 | tf_op jit(solution)/shard_map/ppermute | solution.py:309
  16.1 2.7 %collective-permute-done.6.refs_7_ = f32[392,128]{1,0:T(8,128)S(1)} collective-permute-done((f32[392,128]{1,0:T(8,128)S(1)}, f32[392,128]{1,0:T(8,128)S(1)}, u32[]{:S(2)}, u32[]{:S(2)}) %collective-permute-start.6) | collective-permute-done | bytes 200736 | tf_op jit(solution)/shard_map/ppermute | solution.py:309
  18.9 0.1 pick_masks.1
  19.0 0.0 collective-permute-done.1.refs_2_
  19.0 0.0 collective-permute-done.refs_1_
  19.0 0.0 collective-permute-done.5.refs_6_
  19.0 0.0 collective-permute-done.4.refs_4_
  19.0 1.0 %kernel_sums.1 = f32[64,128]{1,0:T(8,128)S(1)} custom-call(f32[392,128]{1,0:T(8,128)S(1)} %get-tuple-element.15.refs_0_, f32[392,128]{1,0:T(8,128)S(1)} %collective-permute-done.refs_1_, f32[392,128]{1,0:T(8,128)S(1)} %collective-permute-done.1.refs_2_, f32[392,128]{1,0:T(8,128)S(1)} %collective-permute-done.2.refs_3_, ...), custom_call_target="tpu_custom_call" | custom-call | tf_op jit(solution)/shard_map/kernel_sums/pallas_call | solution.py:345
  20.0 9.1 %all_to_all.11 = f32[32,2,128]{2,1,0:T(2,128)S(1)} all-to-all(f32[32,2,128]{2,1,0:T(2,128)S(1)} %bitcast.6), channel_id=1, replica_groups=mesh['row'=4,'col'=8] {'row','col'}, dimensions={0} | all-to-all | bytes 65536 | tf_op jit(solution)/shard_map/all_to_all | solution.py:359
  29.2 0.8 %pick_proof.1 = (f32[1,64]{1,0:T(1,128)}, f32[1,1]{1,0:T(1,128)}) custom-call(f32[64,128]{1,0:T(8,128)S(1)} %bitcast.7, bf16[128,192]{1,0:T(8,128)(2,1)S(1)} %get-tuple-element.22.lane_ref, f32[64,192]{1,0:T(8,128)S(1)} %get-tuple-element.23.row_ref), custom_call_target="tpu_custom_call" | custom-call | tf_op jit(solution)/shard_map/pick_proof/pallas_call | solution.py:361
Async XLA Ops:
  1.7 13.5 %collective-permute-start.3 = (f32[392,128]{1,0:T(8,128)S(1)}, f32[392,128]{1,0:T(8,128)S(1)}, u32[]{:S(2)}, u32[]{:S(2)}) collective-permute-start(f32[392,128]{1,0:T(8,128)S(1)} %get-tuple-element.15.refs_0_), channel_id=1, source_target_pairs={{0,24},{1,25},{2,26},{3,27},{4,28},{5,29},{6,30},{7,31},{8,16},{9,... | collective-permute-start | bytes 602120 | tf_op jit(solution)/shard_map/ppermute | solution.py:309
  6.8 8.8 %collective-permute-start.2 = (f32[392,128]{1,0:T(8,128)S(1)}, f32[392,128]{1,0:T(8,128)S(1)}, u32[]{:S(2)}, u32[]{:S(2)}) collective-permute-start(f32[392,128]{1,0:T(8,128)S(1)} %get-tuple-element.15.refs_0_), channel_id=1, source_target_pairs={{0,6},{1,7},{2,4},{3,5},{4,2},{5,3},{6,0},{7,1},{8,14},{9,15},{10,... | collective-permute-start | bytes 602120 | tf_op jit(solution)/shard_map/ppermute | solution.py:309
  9.3 9.6 %collective-permute-start.6 = (f32[392,128]{1,0:T(8,128)S(1)}, f32[392,128]{1,0:T(8,128)S(1)}, u32[]{:S(2)}, u32[]{:S(2)}) collective-permute-start(f32[392,128]{1,0:T(8,128)S(1)} %get-tuple-element.15.refs_0_), channel_id=1, source_target_pairs={{0,8},{1,9},{2,10},{3,11},{4,12},{5,13},{6,14},{7,15},{8,1},{9,0},... | collective-permute-start | bytes 602120 | tf_op jit(solution)/shard_map/ppermute | solution.py:309
  9.3 9.7 %collective-permute-start.1 = (f32[392,128]{1,0:T(8,128)S(1)}, f32[392,128]{1,0:T(8,128)S(1)}, u32[]{:S(2)}, u32[]{:S(2)}) collective-permute-start(f32[392,128]{1,0:T(8,128)S(1)} %get-tuple-element.15.refs_0_), channel_id=1, source_target_pairs={{0,4},{1,5},{2,6},{3,7},{4,0},{5,1},{6,2},{7,3},{8,12},{9,13},{10,... | collective-permute-start | bytes 602120 | tf_op jit(solution)/shard_map/ppermute | solution.py:309
  9.8 9.2 %collective-permute-start = (f32[392,128]{1,0:T(8,128)S(1)}, f32[392,128]{1,0:T(8,128)S(1)}, u32[]{:S(2)}, u32[]{:S(2)}) collective-permute-start(f32[392,128]{1,0:T(8,128)S(1)} %get-tuple-element.15.refs_0_), channel_id=1, source_target_pairs={{0,2},{1,3},{2,0},{3,1},{4,6},{5,7},{6,4},{7,5},{8,10},{9,11},{10,... | collective-permute-start | bytes 602120 | tf_op jit(solution)/shard_map/ppermute | solution.py:309
  15.6 3.4 %collective-permute-start.5 = (f32[392,128]{1,0:T(8,128)S(1)}, f32[392,128]{1,0:T(8,128)S(1)}, u32[]{:S(2)}, u32[]{:S(2)}) collective-permute-start(f32[392,128]{1,0:T(8,128)S(1)} %collective-permute-done.3.refs_5_), channel_id=1, source_target_pairs={{0,1},{1,0},{2,3},{3,2},{4,5},{5,4},{6,7},{7,6},{8,9},{9,8},{10,11... | collective-permute-start | bytes 602120 | tf_op jit(solution)/shard_map/ppermute | solution.py:309
  15.6 3.4 %collective-permute-start.4 = (f32[392,128]{1,0:T(8,128)S(1)}, f32[392,128]{1,0:T(8,128)S(1)}, u32[]{:S(2)}, u32[]{:S(2)}) collective-permute-start(f32[392,128]{1,0:T(8,128)S(1)} %get-tuple-element.15.refs_0_), channel_id=1, source_target_pairs={{0,1},{1,0},{2,3},{3,2},{4,5},{5,4},{6,7},{7,6},{8,9},{9,8},{10,11... | collective-permute-start | bytes 602120 | tf_op jit(solution)/shard_map/ppermute | solution.py:309

commit v10 on v9

--- a/solution.py
+++ b/solution.py
@@ -327,7 +327,7 @@
     late, *_ = lax.optimization_barrier((packed, in_plane[-1], far_a))
     near = send(late, to_core)
 
-    ids, far_b = lax.optimization_barrier((ids, far_b))
+    ids, far_b, *_ = lax.optimization_barrier((ids, far_b, in_plane[0]))
     lanes, rows = pl.pallas_call(
         functools.partial(pick_kernel, layout, per_peer, factor),
         out_shape=(

time: 30.1 us -> 30.3 us (level)
  no operation moved by 1% of the time
where the time goes in v10:
time: 30.3 us; the launch traced here: 30.1 us
  blocking collectives  9.32 us (31%)
  starting transfers between devices  9.1 us (30%)
  waiting for transfers between devices  8.08 us (27%)
  Pallas kernels  2.94 us (10%)
  between operations  0.67 us (2%)
    all_to_all x1, blocking collectives, local(): lax.all_to_all(partial, ('row', 'col'), split_axis=0, concat_axis=0, tile...  9.32 us
    ppermute x7, starting transfers between devices, send(): return lax.ppermute(block, ('row', 'col'), layout.pairs(target))  9.1 us
    ppermute x7, waiting for transfers between devices, send(): return lax.ppermute(block, ('row', 'col'), layout.pairs(target))  8.08 us
    pallas_call x1, Pallas kernels, local(): pl.pallas_call(pack_kernel, out_shape=(pltpu.VMEM((pack_rows, LANES), jnp...  1.07 us
    pallas_call x1, Pallas kernels, local(): pl.pallas_call(functools.partial(main_kernel, samples, chunks, layout), o...  1.01 us
    pallas_call x1, Pallas kernels, local(): pl.pallas_call(functools.partial(last_kernel, layout, per_peer, factor /...  0.76 us
  transfers between devices with their start and end apart: 7, of which 3 were waited for; matrix products, arithmetic and copies ran while one was open for 0% of the time, Pallas kernels for 0%

profile of v10, /device:TPU:0, one launch (start us, length us, event | category | flops | bytes accessed | tf_op | source)
XLA Modules:
  0.0 30.1 jit_solution(13228869852998042721)
XLA Ops:
  0.6 1.1 %pack_block.1 = (f32[392,128]{1,0:T(8,128)S(1)}, s32[1,64]{1,0:T(1,128)S(1)}) custom-call(f32[64,768]{1,0:T(8,128)} %emb_ref.1, s32[1,64]{1,0:T(1,128)} %bitcast.8, s32[1,64]{1,0:T(1,128)} %bitcast.9), custom_call_target="tpu_custom_call" | custom-call | tf_op jit(solution)/shard_map/pack_block/pallas_call | solution.py:288
  1.7 5.1 %collective-permute-start.3 = (f32[392,128]{1,0:T(8,128)S(1)}, f32[392,128]{1,0:T(8,128)S(1)}, u32[]{:S(2)}, u32[]{:S(2)}) collective-permute-start(f32[392,128]{1,0:T(8,128)S(1)} %get-tuple-element.15.refs_0_), channel_id=1, source_target_pairs={{0,24},{1,25},{2,26},{3,27},{4,28},{5,29},{6,30},{7,31},{8,16},{9,... | collective-permute-start | bytes 602120 | tf_op jit(solution)/shard_map/ppermute | solution.py:309
  6.8 2.4 %collective-permute-start.2 = (f32[392,128]{1,0:T(8,128)S(1)}, f32[392,128]{1,0:T(8,128)S(1)}, u32[]{:S(2)}, u32[]{:S(2)}) collective-permute-start(f32[392,128]{1,0:T(8,128)S(1)} %get-tuple-element.15.refs_0_), channel_id=1, source_target_pairs={{0,6},{1,7},{2,4},{3,5},{4,2},{5,3},{6,0},{7,1},{8,14},{9,15},{10,... | collective-permute-start | bytes 602120 | tf_op jit(solution)/shard_map/ppermute | solution.py:309
  9.3 0.0 collective-permute-start.6
  9.3 0.5 %collective-permute-start = (f32[392,128]{1,0:T(8,128)S(1)}, f32[392,128]{1,0:T(8,128)S(1)}, u32[]{:S(2)}, u32[]{:S(2)}) collective-permute-start(f32[392,128]{1,0:T(8,128)S(1)} %get-tuple-element.15.refs_0_), channel_id=1, source_target_pairs={{0,2},{1,3},{2,0},{3,1},{4,6},{5,7},{6,4},{7,5},{8,10},{9,11},{10,... | collective-permute-start | bytes 602120 | tf_op jit(solution)/shard_map/ppermute | solution.py:309
  9.8 0.5 %collective-permute-start.1 = (f32[392,128]{1,0:T(8,128)S(1)}, f32[392,128]{1,0:T(8,128)S(1)}, u32[]{:S(2)}, u32[]{:S(2)}) collective-permute-start(f32[392,128]{1,0:T(8,128)S(1)} %get-tuple-element.15.refs_0_), channel_id=1, source_target_pairs={{0,4},{1,5},{2,6},{3,7},{4,0},{5,1},{6,2},{7,3},{8,12},{9,13},{10,... | collective-permute-start | bytes 602120 | tf_op jit(solution)/shard_map/ppermute | solution.py:309
  10.3 4.9 %collective-permute-done.3.refs_5_ = f32[392,128]{1,0:T(8,128)S(1)} collective-permute-done((f32[392,128]{1,0:T(8,128)S(1)}, f32[392,128]{1,0:T(8,128)S(1)}, u32[]{:S(2)}, u32[]{:S(2)}) %collective-permute-start.3) | collective-permute-done | bytes 200736 | tf_op jit(solution)/shard_map/ppermute | solution.py:309
  15.2 0.4 %collective-permute-done.2.refs_3_ = f32[392,128]{1,0:T(8,128)S(1)} collective-permute-done((f32[392,128]{1,0:T(8,128)S(1)}, f32[392,128]{1,0:T(8,128)S(1)}, u32[]{:S(2)}, u32[]{:S(2)}) %collective-permute-start.2) | collective-permute-done | bytes 200736 | tf_op jit(solution)/shard_map/ppermute | solution.py:309
  15.6 0.0 collective-permute-start.5
  15.6 0.5 %collective-permute-start.4 = (f32[392,128]{1,0:T(8,128)S(1)}, f32[392,128]{1,0:T(8,128)S(1)}, u32[]{:S(2)}, u32[]{:S(2)}) collective-permute-start(f32[392,128]{1,0:T(8,128)S(1)} %get-tuple-element.15.refs_0_), channel_id=1, source_target_pairs={{0,1},{1,0},{2,3},{3,2},{4,5},{5,4},{6,7},{7,6},{8,9},{9,8},{10,11... | collective-permute-start | bytes 602120 | tf_op jit(solution)/shard_map/ppermute | solution.py:309
  16.1 2.7 %collective-permute-done.6.refs_7_ = f32[392,128]{1,0:T(8,128)S(1)} collective-permute-done((f32[392,128]{1,0:T(8,128)S(1)}, f32[392,128]{1,0:T(8,128)S(1)}, u32[]{:S(2)}, u32[]{:S(2)}) %collective-permute-start.6) | collective-permute-done | bytes 200736 | tf_op jit(solution)/shard_map/ppermute | solution.py:309
  18.9 0.0 collective-permute-done.refs_1_
  18.9 0.1 pick_masks.1
  19.0 0.0 collective-permute-done.1.refs_2_
  19.0 0.0 collective-permute-done.5.refs_6_
  19.0 0.0 collective-permute-done.4.refs_4_
  19.0 1.0 %kernel_sums.1 = f32[64,128]{1,0:T(8,128)S(1)} custom-call(f32[392,128]{1,0:T(8,128)S(1)} %get-tuple-element.15.refs_0_, f32[392,128]{1,0:T(8,128)S(1)} %collective-permute-done.refs_1_, f32[392,128]{1,0:T(8,128)S(1)} %collective-permute-done.1.refs_2_, f32[392,128]{1,0:T(8,128)S(1)} %collective-permute-done.2.refs_3_, ...), custom_call_target="tpu_custom_call" | custom-call | tf_op jit(solution)/shard_map/kernel_sums/pallas_call | solution.py:345
  20.0 9.3 %all_to_all.11 = f32[32,2,128]{2,1,0:T(2,128)S(1)} all-to-all(f32[32,2,128]{2,1,0:T(2,128)S(1)} %bitcast.6), channel_id=1, replica_groups=mesh['row'=4,'col'=8] {'row','col'}, dimensions={0} | all-to-all | bytes 65536 | tf_op jit(solution)/shard_map/all_to_all | solution.py:359
  29.4 0.8 %pick_proof.1 = (f32[1,64]{1,0:T(1,128)}, f32[1,1]{1,0:T(1,128)}) custom-call(f32[64,128]{1,0:T(8,128)S(1)} %bitcast.7, bf16[128,192]{1,0:T(8,128)(2,1)S(1)} %get-tuple-element.22.lane_ref, f32[64,192]{1,0:T(8,128)S(1)} %get-tuple-element.23.row_ref), custom_call_target="tpu_custom_call" | custom-call | tf_op jit(solution)/shard_map/pick_proof/pallas_call | solution.py:361
Async XLA Ops:
  1.7 13.5 %collective-permute-start.3 = (f32[392,128]{1,0:T(8,128)S(1)}, f32[392,128]{1,0:T(8,128)S(1)}, u32[]{:S(2)}, u32[]{:S(2)}) collective-permute-start(f32[392,128]{1,0:T(8,128)S(1)} %get-tuple-element.15.refs_0_), channel_id=1, source_target_pairs={{0,24},{1,25},{2,26},{3,27},{4,28},{5,29},{6,30},{7,31},{8,16},{9,... | collective-permute-start | bytes 602120 | tf_op jit(solution)/shard_map/ppermute | solution.py:309
  6.8 8.8 %collective-permute-start.2 = (f32[392,128]{1,0:T(8,128)S(1)}, f32[392,128]{1,0:T(8,128)S(1)}, u32[]{:S(2)}, u32[]{:S(2)}) collective-permute-start(f32[392,128]{1,0:T(8,128)S(1)} %get-tuple-element.15.refs_0_), channel_id=1, source_target_pairs={{0,6},{1,7},{2,4},{3,5},{4,2},{5,3},{6,0},{7,1},{8,14},{9,15},{10,... | collective-permute-start | bytes 602120 | tf_op jit(solution)/shard_map/ppermute | solution.py:309
  9.3 9.6 %collective-permute-start.6 = (f32[392,128]{1,0:T(8,128)S(1)}, f32[392,128]{1,0:T(8,128)S(1)}, u32[]{:S(2)}, u32[]{:S(2)}) collective-permute-start(f32[392,128]{1,0:T(8,128)S(1)} %get-tuple-element.15.refs_0_), channel_id=1, source_target_pairs={{0,8},{1,9},{2,10},{3,11},{4,12},{5,13},{6,14},{7,15},{8,1},{9,0},... | collective-permute-start | bytes 602120 | tf_op jit(solution)/shard_map/ppermute | solution.py:309
  9.3 9.6 %collective-permute-start = (f32[392,128]{1,0:T(8,128)S(1)}, f32[392,128]{1,0:T(8,128)S(1)}, u32[]{:S(2)}, u32[]{:S(2)}) collective-permute-start(f32[392,128]{1,0:T(8,128)S(1)} %get-tuple-element.15.refs_0_), channel_id=1, source_target_pairs={{0,2},{1,3},{2,0},{3,1},{4,6},{5,7},{6,4},{7,5},{8,10},{9,11},{10,... | collective-permute-start | bytes 602120 | tf_op jit(solution)/shard_map/ppermute | solution.py:309
  9.8 9.2 %collective-permute-start.1 = (f32[392,128]{1,0:T(8,128)S(1)}, f32[392,128]{1,0:T(8,128)S(1)}, u32[]{:S(2)}, u32[]{:S(2)}) collective-permute-start(f32[392,128]{1,0:T(8,128)S(1)} %get-tuple-element.15.refs_0_), channel_id=1, source_target_pairs={{0,4},{1,5},{2,6},{3,7},{4,0},{5,1},{6,2},{7,3},{8,12},{9,13},{10,... | collective-permute-start | bytes 602120 | tf_op jit(solution)/shard_map/ppermute | solution.py:309
  15.6 3.4 %collective-permute-start.5 = (f32[392,128]{1,0:T(8,128)S(1)}, f32[392,128]{1,0:T(8,128)S(1)}, u32[]{:S(2)}, u32[]{:S(2)}) collective-permute-start(f32[392,128]{1,0:T(8,128)S(1)} %collective-permute-done.3.refs_5_), channel_id=1, source_target_pairs={{0,1},{1,0},{2,3},{3,2},{4,5},{5,4},{6,7},{7,6},{8,9},{9,8},{10,11... | collective-permute-start | bytes 602120 | tf_op jit(solution)/shard_map/ppermute | solution.py:309
  15.6 3.4 %collective-permute-start.4 = (f32[392,128]{1,0:T(8,128)S(1)}, f32[392,128]{1,0:T(8,128)S(1)}, u32[]{:S(2)}, u32[]{:S(2)}) collective-permute-start(f32[392,128]{1,0:T(8,128)S(1)} %get-tuple-element.15.refs_0_), channel_id=1, source_target_pairs={{0,1},{1,0},{2,3},{3,2},{4,5},{5,4},{6,7},{7,6},{8,9},{9,8},{10,11... | collective-permute-start | bytes 602120 | tf_op jit(solution)/shard_map/ppermute | solution.py:309
